TPU v7x, 256 devices: a whole 4x4x8 slice. The times are simulated.
256 devices in a mesh: section: 8 (over x_lo, y), tensor: 32 (over z, x_hi, core).
Axes of the slice: x: 4 (x_hi: 2, x_lo: 2; x = x_hi * 2 + x_lo), y: 4, z: 8, core: 2. Of those that a mesh axis runs over, the one named last changes fastest.
Arguments:
- fwd_in: bfloat16 [8, 256, 8192], P('section', 'tensor'), may hold values from -6 to 6
- saved_in: bfloat16 [8, 256, 8192], P('section', 'tensor'), may hold values from -6 to 6
- grad_in: bfloat16 [8, 256, 8192], P('section', 'tensor'), may hold values from -6 to 6
- norm_gain: float32 [8, 8192], P('section'), may hold values from 0.5 to 1.5
- query_weight: bfloat16 [8, 8192, 8192], P('section', None, 'tensor'), may hold values from -2 to 2
- keyval_weight: bfloat16 [8, 8192, 2048], P('section', None, 'tensor'), may hold values from -1 to 1
- out_weight: bfloat16 [8, 8192, 8192], P('section', 'tensor'), may hold values from -0.0625 to 0.0625
- encoder: float32 [64, 128, 32], replicated, may hold values from -0.5 to 0.5
- decoder: float32 [64, 32, 128], replicated, may hold values from -1 to 1
- seq_pos: int32 [256], replicated, may hold values from 0 to 255, each once
- rope_ids: int32 [256], replicated, may hold values from 0 to 4095
Outputs:
- section_out: bfloat16 [8, 256, 8192], P('section', 'tensor')
- act_sent: bfloat16 [8, 256, 8192], P('section', 'tensor')
- input_grad: bfloat16 [8, 256, 8192], P('section', 'tensor')
- grad_sent: bfloat16 [8, 256, 8192], P('section', 'tensor')
Inputs may be any that keep to these rules, and one draw needn't show every extreme that they name: `seq_pos`: a permutation of the 256 positions.
All inputs are finite; a program needn't handle non-finite values.
Results may differ from a plain program's by a relative error of at most 0.022.
Values may be sent and summed in bfloat16 or wider, within the bound.
A program may use at most 128 MiB of HBM per device.

v0:
```python
import math

import jax
import jax.numpy as jnp
from jax import lax
from jax.sharding import PartitionSpec as P

HD = 128
KVH = 8


EPSILON = 1e-05
ROPE_BASE = 10000.0
NEG_FILL = -1e30


def from_partner(x, axis, stride):
    return lax.ppermute(x, axis, [(i, i ^ 1 << stride) for i in range(lax.axis_size(axis))])


def passed_along(x, axis, by):
    peers = lax.axis_size(axis)
    pairs = [(i, i + by) for i in range(peers) if 0 <= i + by < peers]
    return lax.ppermute(x, axis, pairs)


def angle_tables(position_ids, head_size):
    pair_index = jnp.arange(head_size // 2, dtype=jnp.float32)
    frequency = ROPE_BASE ** (-2.0 * pair_index / head_size)
    angle_grid = position_ids.astype(jnp.float32)[:, None] * frequency[None, :]
    return (jnp.cos(angle_grid), jnp.sin(angle_grid))


def rotate_heads(values, cosine, sine_part):
    shaped = values.reshape(values.shape[0], values.shape[1], -1, 2)
    even_part = shaped[..., 0]
    odd_part = shaped[..., 1]
    cos_grid = cosine[:, None, :]
    sin_grid = sine_part[:, None, :]
    turned = jnp.stack(
        [even_part * cos_grid - odd_part * sin_grid, odd_part * cos_grid + even_part * sin_grid],
        axis=-1,
    )
    return turned.reshape(values.shape)


def rotate_columns(values, cosine, sine_part):
    shaped = values.reshape(values.shape[0], -1, 2)
    even_part = shaped[..., 0]
    odd_part = shaped[..., 1]
    turned = jnp.stack(
        [even_part * cosine - odd_part * sine_part, odd_part * cosine + even_part * sine_part],
        axis=-1,
    )
    return turned.reshape(values.shape)


def encode_blocks(values, encoder):
    grouped = values.reshape(values.shape[0], encoder.shape[0], -1)
    mapped = jnp.einsum("tbi,bio->tbo", grouped, encoder, precision=lax.Precision.HIGHEST)
    return mapped.reshape(values.shape[0], -1)


def decode_blocks(values, decoder):
    grouped = values.reshape(values.shape[0], decoder.shape[0], -1)
    mapped = jnp.einsum("tbi,bio->tbo", grouped, decoder, precision=lax.Precision.HIGHEST)
    return mapped.reshape(values.shape[0], -1)


def normalize(activation, gain_row):
    floated = activation.astype(jnp.float32)
    factor = lax.rsqrt(jnp.mean(floated * floated, axis=-1, keepdims=True) + EPSILON)
    return (floated, factor, (floated * factor * gain_row).astype(jnp.bfloat16))


def on_device(
    fwd_in,
    saved_in,
    grad_in,
    norm_gain,
    query_weight,
    keyval_weight,
    out_weight,
    encoder,
    decoder,
    seq_pos,
    rope_ids,
):
    gain_row = norm_gain[0]
    query_matrix = query_weight[0]
    keyval_matrix = keyval_weight[0]
    out_matrix = out_weight[0]
    position = lax.axis_index("tensor")
    tensor_count = lax.axis_size("tensor")
    heads_here = query_matrix.shape[1] // HD
    kv_width = keyval_matrix.shape[1]
    share_count = tensor_count // KVH
    share_bits = share_count.bit_length() - 1
    cosine, sine_part = angle_tables(rope_ids, HD)
    column = position * kv_width + jnp.arange(kv_width, dtype=jnp.int32)
    pair_start = (column % (2 * HD))[::2]
    is_key = pair_start < HD
    pair_index = (pair_start % HD // 2).astype(jnp.float32)
    frequency = ROPE_BASE ** (-2.0 * pair_index / HD)
    angle_grid = rope_ids.astype(jnp.float32)[:, None] * frequency[None, :]
    column_cos = jnp.where(is_key[None, :], jnp.cos(angle_grid), 1.0)
    column_sin = jnp.where(is_key[None, :], jnp.sin(angle_grid), 0.0)

    def reduce_rows(encoded):
        return lax.psum_scatter(
            encoded.astype(jnp.bfloat16), "tensor", scatter_dimension=0, tiled=True
        ).astype(jnp.float32)

    def project_rows(row_piece):
        query_part = jnp.dot(row_piece, query_matrix, preferred_element_type=jnp.float32)
        keyval_part = jnp.dot(row_piece, keyval_matrix, preferred_element_type=jnp.float32)
        return jnp.concatenate([query_part, keyval_part], axis=1)

    def forward_parts(activation_rows):
        floated, factor, normed = normalize(activation_rows, gain_row)
        projected = project_rows(lax.all_gather(normed, "tensor", axis=0, tiled=True))
        tokens = projected.shape[0]
        query_raw = projected[:, : heads_here * HD].reshape(tokens, heads_here, HD)
        query = rotate_heads(query_raw, cosine, sine_part).astype(jnp.bfloat16)
        keyval_local = rotate_columns(
            projected[:, heads_here * HD :], column_cos, column_sin
        ).astype(jnp.bfloat16)
        head_cols = keyval_local
        for bit_index in range(share_bits):
            partner = from_partner(head_cols, "tensor", bit_index)
            lower_side = position // 2**bit_index % 2 == 0
            head_cols = jnp.where(
                lower_side,
                jnp.concatenate([head_cols, partner], axis=1),
                jnp.concatenate([partner, head_cols], axis=1),
            )
        key_rows = head_cols[:, :HD]
        value_rows = head_cols[:, HD:]
        scores = jnp.einsum(
            "thd,sd->hts", query, key_rows, preferred_element_type=jnp.float32
        ) / math.sqrt(HD)
        visible = seq_pos[None, :] <= seq_pos[:, None]
        masked = jnp.where(visible[None], scores, NEG_FILL)
        highest = jnp.max(masked, axis=-1, keepdims=True)
        raised = jnp.exp(masked - highest)
        weighting = raised / jnp.sum(raised, axis=-1, keepdims=True)
        rounded_weighting = weighting.astype(jnp.bfloat16)
        attended = jnp.einsum(
            "hts,sd->thd", rounded_weighting, value_rows, preferred_element_type=jnp.float32
        )
        attended = attended.astype(jnp.bfloat16).reshape(tokens, heads_here * HD)
        return (
            floated,
            factor,
            query,
            key_rows,
            value_rows,
            weighting,
            rounded_weighting,
            attended,
        )

    floated, factor, query, key_rows, value_rows, weighting, rounded_weighting, attended = (
        forward_parts(fwd_in[0])
    )
    partial_value = jnp.dot(attended, out_matrix, preferred_element_type=jnp.float32)
    delta_rows = decode_blocks(reduce_rows(encode_blocks(partial_value, encoder)), decoder)
    section_out = (floated + delta_rows).astype(jnp.bfloat16)
    packed = encode_blocks(section_out.astype(jnp.float32), encoder).astype(jnp.bfloat16)
    arrived = passed_along(packed, "section", 1)
    act_sent = decode_blocks(arrived.astype(jnp.float32), decoder).astype(jnp.bfloat16)
    section_out, act_sent = (section_out, act_sent)
    floated, factor, query, key_rows, value_rows, weighting, rounded_weighting, attended = (
        forward_parts(saved_in[0])
    )
    tokens = query.shape[0]
    grad_att = jnp.einsum(
        "td,kd->tk",
        lax.all_gather(grad_in[0], "tensor", axis=0, tiled=True),
        out_matrix,
        preferred_element_type=jnp.float32,
    )
    grad_att = grad_att.astype(jnp.bfloat16).reshape(tokens, heads_here, HD)
    prob_grad = jnp.einsum("thd,sd->hts", grad_att, value_rows, preferred_element_type=jnp.float32)
    score_grad = (
        weighting
        * (prob_grad - jnp.sum(weighting * prob_grad, axis=-1, keepdims=True))
        / math.sqrt(HD)
    )
    score_grad = score_grad.astype(jnp.bfloat16)
    query_grad = jnp.einsum("hts,sd->thd", score_grad, key_rows, preferred_element_type=jnp.float32)
    query_grad = rotate_heads(query_grad, cosine, -sine_part).astype(jnp.bfloat16)
    key_grad = jnp.einsum("hts,thd->sd", score_grad, query, preferred_element_type=jnp.float32)
    key_grad = rotate_heads(key_grad[:, None, :], cosine, -sine_part)[:, 0, :]
    value_grad = jnp.einsum(
        "hts,thd->sd", rounded_weighting, grad_att, preferred_element_type=jnp.float32
    )
    head_grad = jnp.concatenate([key_grad, value_grad], axis=1)
    for bit_index in reversed(range(share_bits)):
        half_width = head_grad.shape[1] // 2
        lower_side = position // 2**bit_index % 2 == 0
        kept_part = jnp.where(lower_side, head_grad[:, :half_width], head_grad[:, half_width:])
        sent_part = jnp.where(lower_side, head_grad[:, half_width:], head_grad[:, :half_width])
        head_grad = kept_part + from_partner(
            sent_part.astype(jnp.bfloat16), "tensor", bit_index
        ).astype(sent_part.dtype)
    keyval_grad = head_grad.astype(jnp.bfloat16)
    normed_grad = jnp.einsum(
        "tk,dk->td",
        query_grad.reshape(tokens, heads_here * HD),
        query_matrix,
        preferred_element_type=jnp.float32,
    )
    normed_grad = normed_grad + jnp.einsum(
        "tk,dk->td", keyval_grad, keyval_matrix, preferred_element_type=jnp.float32
    )
    recovered = decode_blocks(reduce_rows(encode_blocks(normed_grad, encoder)), decoder)
    scaled = recovered * gain_row
    correction = factor * (
        scaled - floated * factor * factor * jnp.mean(scaled * floated, axis=-1, keepdims=True)
    )
    input_grad = (grad_in[0].astype(jnp.float32) + correction).astype(jnp.bfloat16)
    packed = encode_blocks(input_grad.astype(jnp.float32), encoder).astype(jnp.bfloat16)
    arrived = passed_along(packed, "section", -1)
    grad_sent = decode_blocks(arrived.astype(jnp.float32), decoder).astype(jnp.bfloat16)
    input_grad, grad_sent = (input_grad, grad_sent)
    return (section_out[None], act_sent[None], input_grad[None], grad_sent[None])


def solution(mesh):
    return jax.shard_map(
        on_device,
        mesh=mesh,
        in_specs=(
            P("section", "tensor", None),
            P("section", "tensor", None),
            P("section", "tensor", None),
            P("section", None),
            P("section", None, "tensor"),
            P("section", None, "tensor"),
            P("section", "tensor", None),
            P(),
            P(),
            P(),
            P(),
        ),
        out_specs=(
            P("section", "tensor", None),
            P("section", "tensor", None),
            P("section", "tensor", None),
            P("section", "tensor", None),
        ),
        check_vma=False,
    )
```

profile of v0, /device:TPU:2, one launch (start us, length us, event | category | flops | bytes accessed | tf_op | source)
XLA Modules:
  0.0 557.3 jit_solution(8924904743498269585)
XLA Ops:
  7.2 1.2 fusion.67
  8.4 1.1 fusion.70
  9.5 1.8 fusion.69
  11.4 0.7 all-gather.5.cloned.1.call-update
  12.1 0.7 all-gather.9.cloned.1.call-update
  12.9 1.7 dot_general.86
  14.8 0.7 convert_element_type.206
  15.5 6.4 %copy.33 = bf16[256,8192]{1,0:T(8,128)(2,1)} copy(bf16[256,8192]{0,1:T(8,128)(2,1)} %bitcast.239) | data formatting | bytes 8388608 | tf_op jit(solution)/shard_map/dot_general | solution.py:115
  21.8 7.7 %dot_general.89 = bf16[2,64,2,8192]{3,2,1,0:T(2,128)(2,1)} reshape(bf16[256,8192]{1,0:T(8,128)(2,1)} %copy.33) | data formatting | bytes 8388608 | tf_op jit(solution)/shard_map/dot_general | solution.py:115
  29.7 0.3 fusion.134
  30.0 70.3 %all-gather.7.cloned.1.call-done = bf16[256,8192]{1,0:T(8,128)(2,1)} async-done(((bf16[8,8192]{1,0:T(8,128)(2,1)}), bf16[256,8192]{1,0:T(8,128)(2,1)}) %all-gather.7.cloned.1.call-update) | async-done | bytes 4194320 | tf_op jit(solution)/shard_map/all_gather | solution.py:121
  100.3 3.5 fusion.15
  103.9 83.3 %all-gather.5.cloned.1.call-done = bf16[256,8192]{1,0:T(8,128)(2,1)} async-done(((bf16[8,8192]{1,0:T(8,128)(2,1)}), bf16[256,8192]{1,0:T(8,128)(2,1)}) %all-gather.5.cloned.1.call-update) | async-done | bytes 4194320 | tf_op jit(solution)/shard_map/all_gather | solution.py:121
  187.2 3.5 fusion.20
  190.8 0.2 fusion.121
  191.2 0.3 collective-permute-start.3
  191.7 0.9 collective-permute-start
  192.6 8.9 %fusion.11 = f32[256,2,64,2]{0,2,3,1:T(8,128)S(1)} fusion(bf16[256,8192]{1,0:T(8,128)(2,1)} %all-gather.5.cloned.1.call-done, bf16[2,64,2,8192]{3,2,1,0:T(2,128)(2,1)} %dot_general.89), kind=kOutput, calls=%fused_computation.12 | convolution fusion | flops 1073741824 | bytes 8650752 | tf_op jit(solution)/shard_map/dot_general | solution.py:115
  201.5 5.0 fusion.9
  206.6 66.9 %all-gather.9.cloned.1.call-done = bf16[1,256,8192]{2,1,0:T(8,128)(2,1)} async-done(((bf16[1,8,8192]{2,1,0:T(8,128)(2,1)}), bf16[1,256,8192]{2,1,0:T(8,128)(2,1)}) %all-gather.9.cloned.1.call-update) | async-done | bytes 4194320 | tf_op jit(solution)/shard_map/all_gather | solution.py:179
  273.5 4.7 fusion.42
  278.6 0.3 maximum_select_fusion.2
  278.9 1.5 collective-permute-start.1
  280.6 2.2 collective-permute-start.4
  282.7 2.1 collective-permute-done.1
  284.9 0.2 fusion.35
  285.1 0.3 fusion.150
  285.4 1.0 collective-permute-done.4
  286.5 1.1 fusion.153
  287.5 0.2 convolution_bitcast_fusion
  287.8 1.5 convolution_bitcast_fusion.1
  289.3 1.5 convolution_bitcast_fusion.3
  290.8 0.3 fusion.106
  291.3 1.3 select_convert_fusion
  292.6 2.2 collective-permute-start.5
  294.8 0.2 copy.54
  295.1 0.3 convolution_convert_fusion.5
  295.4 3.5 fusion.6
  298.8 8.5 %convolution_convert_fusion = bf16[64,256,32]{1,2,0:T(8,128)(2,1)S(1)} fusion(f32[256,64,128]{2,0,1:T(8,128)S(1)} %fusion.6, f32[64,128,32]{1,2,0:T(8,128)S(1)} %copy-done), kind=kOutput, calls=%fused_computation.27 | convolution fusion | flops 805830656 | bytes 10485760 | tf_op jit(solution)/shard_map/tbi,bio->tbo/dot_general | solution.py:60
  307.6 1.4 copy.39
  309.2 0.3 collective-permute-start.6
  309.5 3.5 fusion.18
  313.0 1.3 fusion.24
  314.3 8.5 %fusion.25 = bf16[64,256,32]{1,2,0:T(8,128)(2,1)S(1)} fusion(f32[64,128,32]{1,2,0:T(8,128)S(1)} %copy-done, f32[32,64,8,128]{3,2,1,0:T(8,128)S(1)} %fusion.24), kind=kOutput, calls=%fused_computation.26 | convolution fusion | flops 805830656 | bytes 10485760 | tf_op jit(solution)/shard_map/tbi,bio->tbo/dot_general | solution.py:60
  322.9 1.4 copy.63
  324.3 96.9 %reduce-scatter.3.cloned.1.call-done = bf16[8,2048]{1,0:T(8,128)(2,1)} async-done(((bf16[256,2048]{1,0:T(8,128)(2,1)}), bf16[8,2048]{1,0:T(8,128)(2,1)}) %reduce-scatter.3.cloned.1.call-update) | async-done | bytes 32784 | tf_op jit(solution)/shard_map/reduce_scatter | solution.py:110
  421.2 0.9 reshape.604
  422.1 1.3 fusion.73
  423.4 0.9 fusion.47
  424.4 0.2 convert_element_type.222
  424.6 3.6 collective-permute-start.2
  428.2 4.3 collective-permute-done.2
  432.5 0.1 reshape.606
  432.7 1.3 fusion.41
  434.0 105.0 %reduce-scatter.5.cloned.1.call-done = bf16[8,2048]{1,0:T(8,128)(2,1)} async-done(((bf16[256,2048]{1,0:T(8,128)(2,1)}), bf16[8,2048]{1,0:T(8,128)(2,1)}) %reduce-scatter.5.cloned.1.call-update) | async-done | bytes 32784 | tf_op jit(solution)/shard_map/reduce_scatter | solution.py:110
  538.9 0.9 reshape.611
  539.9 0.8 fusion.62
  540.7 1.0 fusion.48
  541.7 0.2 convert_element_type.253
  541.9 5.6 collective-permute-start.7
  547.4 0.8 fusion.59
  548.2 0.8 collective-permute-done.7
  549.0 0.1 reshape.613
  549.2 1.3 fusion.40
  (68 shorter events, 2.1 us)
Async XLA Ops:
  7.2 291.7 %copy-start = (f32[64,128,32]{1,2,0:T(8,128)S(1)}, f32[64,128,32]{1,2,0:T(8,128)}, u32[]{:S(2)}) copy-start(f32[64,128,32]{1,2,0:T(8,128)} %param.18) | copy-start | bytes 3145732
  7.2 93.2 %all-gather.7.cloned.1.call-start = ((), (), s32[]{:S(2)}) async-start(), calls=%async_computation.4 | async-start | bytes 4325376 | tf_op jit(solution)/shard_map/all_gather | solution.py:121
  11.3 175.9 %all-gather.5.cloned.1.call-start = ((), (), s32[]{:S(2)}) async-start(), calls=%async_computation.2 | async-start | bytes 4325376 | tf_op jit(solution)/shard_map/all_gather | solution.py:121
  12.1 261.4 %all-gather.9.cloned.1.call-start = ((), (), s32[]{:S(2)}) async-start(), calls=%async_computation.6 | async-start | bytes 4325376 | tf_op jit(solution)/shard_map/all_gather | solution.py:179
  12.8 408.4 %reduce-scatter.3.cloned.1.call-start = ((), (), s32[]{:S(2)}) async-start(), calls=%async_computation.3 | async-start | bytes 1081344 | tf_op jit(solution)/shard_map/reduce_scatter | solution.py:110
  21.8 7.8 %copy-start.8 = (s32[256]{0:T(256)S(1)}, s32[256]{0:T(256)}, u32[]{:S(2)}) copy-start(s32[256]{0:T(256)} %param.20) | copy-start | bytes 3076
  191.2 89.2 %collective-permute-start.3 = (bf16[256,64]{1,0:T(8,128)(2,1)S(1)}, bf16[256,64]{1,0:T(8,128)(2,1)S(1)}, u32[]{:S(2)}, u32[]{:S(2)}) collective-permute-start(bf16[256,64]{1,0:T(8,128)(2,1)S(1)} %copy.46), channel_id=1, source_target_pairs={{0,1},{1,0},{2,3},{3,2},{4,5},{5,4},{6,7},{7,6},{8,9},{9,8},{10,11... | collective-permute-start | bytes 98312 | tf_op jit(solution)/shard_map/ppermute | solution.py:18
  191.7 9.8 %copy-start.2 = (bf16[2,64,2,8192]{3,2,1,0:T(2,128)(2,1)S(1)}, bf16[2,64,2,8192]{3,2,1,0:T(2,128)(2,1)}, u32[]{:S(2)}) copy-start(bf16[2,64,2,8192]{3,2,1,0:T(2,128)(2,1)} %dot_general.89) | copy-start | bytes 12582916
  191.7 9.8 %copy-start.9 = (bf16[256,8192]{1,0:T(8,128)(2,1)S(1)}, bf16[256,8192]{1,0:T(8,128)(2,1)}, u32[]{:S(2)}) copy-start(bf16[256,8192]{1,0:T(8,128)(2,1)} %all-gather.7.cloned.1.call-done) | copy-start | bytes 12582916
  191.7 86.9 %collective-permute-start = (bf16[256,64]{1,0:T(8,128)(2,1)S(1)}, bf16[256,64]{1,0:T(8,128)(2,1)S(1)}, u32[]{:S(2)}, u32[]{:S(2)}) collective-permute-start(bf16[256,64]{1,0:T(8,128)(2,1)S(1)} %copy.31), channel_id=1, source_target_pairs={{0,1},{1,0},{2,3},{3,2},{4,5},{5,4},{6,7},{7,6},{8,9},{9,8},{10,11... | collective-permute-start | bytes 98312 | tf_op jit(solution)/shard_map/ppermute | solution.py:18
  278.9 6.0 %collective-permute-start.1 = (bf16[256,128]{1,0:T(8,128)(2,1)S(1)}, bf16[256,128]{1,0:T(8,128)(2,1)S(1)}, u32[]{:S(2)}, u32[]{:S(2)}) collective-permute-start(bf16[256,128]{1,0:T(8,128)(2,1)S(1)} %maximum_select_fusion.2), channel_id=1, source_target_pairs={{0,2},{1,3},{2,0},{3,1},{4,6},{5,7},{6,4},{7,5},{8,10},{9,11},{10,... | collective-permute-start | bytes 196616 | tf_op jit(solution)/shard_map/ppermute | solution.py:18
  280.6 5.9 %collective-permute-start.4 = (bf16[256,128]{1,0:T(8,128)(2,1)S(1)}, bf16[256,128]{1,0:T(8,128)(2,1)S(1)}, u32[]{:S(2)}, u32[]{:S(2)}) collective-permute-start(bf16[256,128]{1,0:T(8,128)(2,1)S(1)} %maximum_select_fusion.3), channel_id=1, source_target_pairs={{0,2},{1,3},{2,0},{3,1},{4,6},{5,7},{6,4},{7,5},{8,10},{9,11},{10,... | collective-permute-start | bytes 196616 | tf_op jit(solution)/shard_map/ppermute | solution.py:18
  292.6 16.5 %collective-permute-start.5 = (bf16[256,128]{0,1:T(8,128)(2,1)S(1)}, bf16[256,128]{0,1:T(8,128)(2,1)S(1)}, u32[]{:S(2)}, u32[]{:S(2)}) collective-permute-start(bf16[256,128]{0,1:T(8,128)(2,1)S(1)} %get-tuple-element.33), channel_id=1, source_target_pairs={{0,2},{1,3},{2,0},{3,1},{4,6},{5,7},{6,4},{7,5},{8,10},{9,11},{10,... | collective-permute-start | bytes 196616 | tf_op jit(solution)/shard_map/ppermute | solution.py:18
  309.1 229.9 %reduce-scatter.5.cloned.1.call-start = ((), (), s32[]{:S(2)}) async-start(), calls=%async_computation.5 | async-start | bytes 1081344 | tf_op jit(solution)/shard_map/reduce_scatter | solution.py:110
  309.2 3.8 copy-start.3
  309.2 3.8 collective-permute-start.6
  314.3 107.8 %copy-start.1 = (f32[64,32,128]{2,1,0:T(8,128)S(1)}, f32[64,32,128]{2,1,0:T(8,128)}, u32[]{:S(2)}) copy-start(f32[64,32,128]{2,1,0:T(8,128)} %param.19) | copy-start | bytes 3145732
  314.3 107.8 %copy-start.5 = (bf16[1,8,8192]{2,1,0:T(8,128)(2,1)S(1)}, bf16[1,8,8192]{2,1,0:T(8,128)(2,1)}, u32[]{:S(2)}) copy-start(bf16[1,8,8192]{2,1,0:T(8,128)(2,1)} %param.11) | copy-start | bytes 393220
  322.9 217.0 %copy-start.4 = (bf16[1,8,8192]{2,1,0:T(8,128)(2,1)S(1)}, bf16[1,8,8192]{2,1,0:T(8,128)(2,1)}, u32[]{:S(2)}) copy-start(bf16[1,8,8192]{2,1,0:T(8,128)(2,1)} %param.12) | copy-start | bytes 393220
  322.9 217.0 %copy-start.7 = (f32[1,8192]{1,0:T(1,128)S(1)}, f32[1,8192]{1,0:T(1,128)}, u32[]{:S(2)}) copy-start(f32[1,8192]{1,0:T(1,128)} %param.14) | copy-start | bytes 98308
  324.3 216.3 %copy-start.6 = (bf16[1,8,8192]{2,1,0:T(8,128)(2,1)S(1)}, bf16[1,8,8192]{2,1,0:T(8,128)(2,1)}, u32[]{:S(2)}) copy-start(bf16[1,8,8192]{2,1,0:T(8,128)(2,1)} %param.13) | copy-start | bytes 393220
  424.6 7.9 %collective-permute-start.2 = (bf16[8,2048]{1,0:T(8,128)(2,1)S(1)}, bf16[8,2048]{1,0:T(8,128)(2,1)S(1)}, u32[]{:S(2)}, u32[]{:S(2)}) collective-permute-start(bf16[8,2048]{1,0:T(8,128)(2,1)S(1)} %convert_element_type.222), channel_id=1, source_target_pairs={{0,32},{32,64},{64,96},{96,128},{128,160},{160,192},{192,224},{1,3... | collective-permute-start | bytes 98312 | tf_op jit(solution)/shard_map/ppermute | solution.py:24
  541.9 7.2 %collective-permute-start.7 = (bf16[8,2048]{1,0:T(8,128)(2,1)S(1)}, bf16[8,2048]{1,0:T(8,128)(2,1)S(1)}, u32[]{:S(2)}, u32[]{:S(2)}) collective-permute-start(bf16[8,2048]{1,0:T(8,128)(2,1)S(1)} %convert_element_type.253), channel_id=1, source_target_pairs={{32,0},{64,32},{96,64},{128,96},{160,128},{192,160},{224,192},{33,... | collective-permute-start | bytes 98312 | tf_op jit(solution)/shard_map/ppermute | solution.py:24
Sparse Core Ops, SparseCore 0:
  11.5 88.8 all-gather.6
  103.7 83.4 all-gather.4
  190.0 83.4 all-gather.8
  309.2 111.9 reduce-scatter.2
  425.7 113.2 reduce-scatter.4
where the time goes:
time: 564 us; the launch traced here: 557 us
  waiting for transfers between devices  432 us (77%)
  matrix products  64 us (11%)
  local copies, waits for them, and re-layouts  22.6 us (4%)
  starting transfers between devices  16.8 us (3%)
  between operations  14.7 us (3%)
  other arithmetic  7.25 us (1%)
    reduce_scatter x2, waiting for transfers between devices, reduce_rows(): lax.psum_scatter(encoded.astype(jnp.bfloat16), 'tensor', scatter_dimensio...  202 us
    all_gather x2, waiting for transfers between devices, forward_parts(): lax.all_gather(normed, 'tensor', axis=0, tiled=True)  154 us
    all_gather x1, waiting for transfers between devices, on_device(): lax.all_gather(grad_in[0], 'tensor', axis=0, tiled=True)  66.9 us
    dot_general x4, matrix products, encode_blocks(): jnp.einsum('tbi,bio->tbo', grouped, encoder, precision=lax.Precision.HIGH...  18.9 us
    dot_general x2, local copies, waits for them, and re-layouts, project_rows(): jnp.dot(row_piece, query_matrix, preferred_element_type=jnp.float32)  14.1 us
    dot_general x2, matrix products, project_rows(): jnp.dot(row_piece, query_matrix, preferred_element_type=jnp.float32)  13.9 us
  transfers between devices with their start and end apart: 13, of which 9 were waited for; matrix products, arithmetic and copies ran while one was open for 14% of the time, Pallas kernels for 0%

commit v1 on v0

v1 whole, which is shorter than its diff:
```python
import math

import jax
import jax.numpy as jnp
from jax import lax
from jax.experimental import pallas as pl
from jax.experimental.pallas import tpu as pltpu
from jax.sharding import PartitionSpec as P

MESH = pl.DeviceIdType.MESH
HD = 128
D = 8192
HALF = D // 2
ENC = 2048
T = 256
EPSILON = 1e-05
ROPE_BASE = 10000.0
NEG_FILL = -1e30
SCALE = 1.0 / math.sqrt(HD)
F32 = jnp.float32
BF16 = jnp.bfloat16
SAVED, GRAD, FWD = 0, 1, 2

KEYS = [(0, 1), (0, -1), (0, 2), (0, -2), (0, 3), (0, -3), (0, 4, 0), (0, 4, 1)]
KEYS += [(1, 0), (1, 1), (1, -1), (1, 2), (1, -2), (1, 3), (1, -3), (1, 4, 0), (1, 4, 1)]
BLOCKS = [(0, 0)] + [k for k in KEYS if len(k) == 2] + [(0, 4), (1, 4)]
GROUPS = [
    ([], [("M", (0, 0), (0, 1)), ("P", (0, 0), (0, -1)), ("X", (0, 0), (1, 0))], [(0, 0)]),
    (
        [(0, 1), (0, -1)],
        [("M", (0, 1), (0, 2)), ("P", (0, -1), (0, -2)), ("X", (0, 1), (1, 1)), ("X", (0, -1), (1, -1))],
        [(0, 1), (0, -1)],
    ),
    ([(1, 0)], [], [(1, 0)]),
    (
        [(0, 2), (0, -2)],
        [("M", (0, 2), (0, 3)), ("P", (0, -2), (0, -3)), ("X", (0, 2), (1, 2)), ("X", (0, -2), (1, -2))],
        [(0, 2), (0, -2)],
    ),
    ([(1, 1), (1, -1)], [], [(1, 1), (1, -1)]),
    ([(0, 3), (0, -3)], [("M", (0, 3), (0, 4, 0)), ("P", (0, -3), (0, 4, 1))], [(0, 3), (0, -3)]),
    ([(1, 2)], [("M", (1, 2), (1, 3))], [(1, 2)]),
    ([(1, -2)], [("P", (1, -2), (1, -3))], [(1, -2)]),
    ([(0, 4, 0), (0, 4, 1)], [], [(0, 4)]),
    ([(1, 3), (1, -3)], [("M", (1, 3), (1, 4, 0)), ("P", (1, -3), (1, 4, 1))], [(1, 3), (1, -3)]),
    ([(1, 4, 0), (1, 4, 1)], [], [(1, 4)]),
]
OFFSETS = (0.0, 4.1, 8.2)
TASKS = [(1.5, "enc"), (4.05, "woe"), (7.05, "qe"), (10.05, "projS"), (12.5, "attS"), (14.15, "gatt"), (14.3, "bwd")]
TASKS += [(15.3, "kvsum"), (15.4, "rsb0"), (16.3, "rsb1"), (19.0, "fwd")]
ORDER = [(i + off, a) for a, off in enumerate(OFFSETS) for i in range(len(GROUPS))] + TASKS
ORDER = [item for _, item in sorted(ORDER, key=lambda entry: entry[0])]


def mm(a, b):
    return jnp.dot(a, b, preferred_element_type=F32)


def mm_nt(a, b):
    return lax.dot_general(a, b, (((1,), (1,)), ((), ())), preferred_element_type=F32)


def rotate(x, cosine, sine):
    lane = lax.broadcasted_iota(jnp.int32, x.shape, 1)
    swapped = jnp.where(lane % 2 == 0, pltpu.roll(x, x.shape[1] - 1, 1), pltpu.roll(x, 1, 1))
    return x * cosine + swapped * sine


def kernel(
    fwd_ref, saved_ref, grad_ref, gain_ref, cos_ref, sin_ref, kvcos_ref, kvsin_ref, seqc_ref, seqr_ref,
    wq_hbm, wkv_hbm, wo_hbm, enc_hbm, dec_hbm,
    out_ref, act_ref, ig_ref, gs_ref,
    G, wq, wkv, wo, enc_raw, dec_raw, enc_bd, enc_t, dec_bd, woe, qe, kve,
    nrm, chipf, factor_ref, accq, acckv, accg, kvt, qrot, qtr, gab, gatr, prob, att, qg, kvg, kgs, kgr,
    rsb, r1, r2, r3, pk_s, pk_r, scaled_ref,
    wsem, st_s, st_r, g_s, g_r, sb_s, sb_r, kv_s, kv_r, kg_s, kg_r, rs_s, rs_r, sc_s, sc_r,
):
    s = lax.axis_index("section")
    t = lax.axis_index("tensor")
    z, h, c = t // 4, (t // 2) % 2, t % 2
    j = t % 4

    def tid(zz, hh, cc):
        return (s, zz * 4 + hh * 2 + cc)

    def zmod(d):
        return lax.rem(z + d + 8, 8)

    sib = tid(z, h, 1 - c)
    link = {"M": tid(zmod(-1), h, c), "P": tid(zmod(1), h, c), "X": tid(z, 1 - h, c)}
    group = [sib, link["X"], tid(z, 1 - h, 1 - c)]
    nxt, prv = (lax.rem(s + 1, 8), t), (lax.rem(s + 7, 8), t)
    along = [tid(zmod(k), h, c) for k in range(1, 8)]

    loads = []
    for i, (src, dst) in enumerate([(enc_hbm, enc_raw), (dec_hbm, dec_raw), (wo_hbm, wo), (wq_hbm, wq), (wkv_hbm, wkv)]):
        loads.append(pltpu.make_async_copy(src, dst, wsem.at[i]))
        loads[-1].start()

    barrier = pltpu.get_barrier_semaphore()
    for peer in along + group + [nxt, prv]:
        pl.semaphore_signal(barrier, inc=1, device_id=peer, device_id_type=MESH)

    def put_own(a, values):
        nrm[a, 0] = values[:, :HALF]
        nrm[a, 1] = values[:, HALF:]

    def normed(ref, slot):
        x = ref[...].astype(F32)
        factor = lax.rsqrt(jnp.mean(x * x, axis=-1, keepdims=True) + EPSILON)
        if slot is not None:
            factor_ref[...] = jnp.broadcast_to(factor, factor_ref.shape)
        return x * factor * gain_ref[...]

    pending = []

    def send(src, dst, ssem, rsem, peer):
        copy = pltpu.make_async_remote_copy(
            src_ref=src, dst_ref=dst, send_sem=ssem, recv_sem=rsem, device_id=peer, device_id_type=MESH
        )
        copy.start()
        pending.append(copy)

    def arrived(dst, ssem, rsem, peer):
        pltpu.make_async_remote_copy(
            src_ref=dst, dst_ref=dst, send_sem=ssem, recv_sem=rsem, device_id=peer, device_id_type=MESH
        ).wait_recv()

    put_own(SAVED, normed(saved_ref, 0))
    pl.semaphore_wait(barrier, len(along) + len(group) + 2)

    def stage(a):
        send(nrm.at[a, 1 - c], chipf.at[a, c], st_s.at[a], st_r.at[a], sib)

    stage(SAVED)
    put_own(GRAD, grad_ref[...].astype(F32))
    stage(GRAD)
    put_own(FWD, normed(fwd_ref, None))
    stage(FWD)

    def where(key):
        column = h if key[0] == 0 else 1 - h
        return column * 8 + zmod(key[1])

    def piece(a, half, key):
        ref = G.at[a, half, where(key)]
        if len(key) == 3:
            ref = ref.at[:, pl.ds(key[2] * (HALF // 2), HALF // 2)]
        return ref

    def form_own(a):
        arrived(chipf.at[a, 1 - c], st_s.at[a], st_r.at[a], sib)
        chipf[a, c] = nrm[a, c]
        G[a, c, h * 8 + z] = chipf[a].reshape(16, HALF).astype(BF16)

    def step(a, g):
        waits, sends, ready = GROUPS[g]
        if g == 0:
            form_own(a)
        for key in waits:
            i = KEYS.index(key)
            arrived(piece(a, c, key), g_s.at[a, i], g_r.at[a, i], link["M"])
        for way, here, there in sends:
            i = KEYS.index(there)
            part = piece(a, c, here + there[2:])
            send(part, part, g_s.at[a, i], g_r.at[a, i], link[way])
        for key in ready:
            i = BLOCKS.index(key)
            send(piece(a, c, key), piece(a, c, key), sb_s.at[a, i], sb_r.at[a, i], sib)

    def whole(a):
        for i, key in enumerate(BLOCKS):
            arrived(piece(a, 1 - c, key), sb_s.at[a, i], sb_r.at[a, i], sib)

    def make_enc():
        loads[0].wait()
        loads[1].wait()

        def fill(i, _):
            e = enc_raw[pl.ds(i * 512, 512), :]
            wide = jnp.concatenate([e, e, e, e], axis=1)
            row = lax.broadcasted_iota(jnp.int32, (512, 128), 0) // 128
            col = lax.broadcasted_iota(jnp.int32, (512, 128), 1) // 32
            wide = jnp.where(row == col, wide, 0.0)
            enc_bd[pl.ds(i * 512, 512), :] = wide.astype(BF16)
            enc_t[pl.ds(i * 128, 128), :] = wide.T.astype(BF16)
            d = dec_raw[pl.ds(i * 128, 128), :]
            drow = lax.broadcasted_iota(jnp.int32, (128, 128), 0) // 32
            parts = [jnp.where(drow == q, d, 0.0) for q in range(4)]
            dec_bd[pl.ds(i * 128, 128), :] = jnp.concatenate(parts, axis=1).astype(BF16)
            return 0

        lax.fori_loop(0, 16, fill, 0)

    def make_woe():
        loads[2].wait()

        def fill(i, _):
            cols = pl.ds(pl.multiple_of(i * 512, 512), 512)
            outs = pl.ds(pl.multiple_of(i * 128, 128), 128)
            woe[:, outs] = mm(wo[:, cols], enc_bd[pl.ds(i * 512, 512), :]).astype(BF16)
            return 0

        lax.fori_loop(0, 16, fill, 0)

    def make_qe():
        loads[3].wait()
        loads[4].wait()

        def fill(i, _):
            rows, outs = pl.ds(i * 512, 512), pl.ds(i * 128, 128)
            e = enc_t[outs, :]
            qe[outs, :] = mm(e, wq[rows, :]).astype(BF16)
            kve[outs, :] = mm(e, wkv[rows, :]).astype(BF16)
            return 0

        lax.fori_loop(0, 16, fill, 0)

    def each_chunk(a, body):
        for half in range(2):

            def chunk(k, _, half=half):
                x = G[a, half, :, :, pl.ds(pl.multiple_of(k * 1024, 1024), 1024)].reshape(T, 1024)
                body(x, pl.multiple_of(half * HALF + k * 1024, 1024))
                return 0

            lax.fori_loop(0, HALF // 1024, chunk, 0)

    def project(a, w):
        whole(a)
        accq[...] = jnp.zeros_like(accq)
        acckv[...] = jnp.zeros_like(acckv)

        def body(x, at):
            accq[...] += mm(x, wq[pl.ds(at, 1024), :])
            acckv[:, :64] += mm(x, wkv[pl.ds(at, 1024), :])

        each_chunk(a, body)
        turned = rotate(acckv[...], kvcos_ref[...], kvsin_ref[...])
        kvt[w, j] = turned.T[:64].astype(BF16)
        for i, peer in enumerate(group):
            send(kvt.at[w, j], kvt.at[w, j], kv_s.at[w, i], kv_r.at[w, i], peer)
        for i in range(2):
            cols = slice(i * HD, (i + 1) * HD)
            q = rotate(accq[:, cols], cos_ref[...], sin_ref[...])
            qrot[:, cols] = q.astype(BF16)
            if w == 0:
                qtr[i] = q.T.astype(BF16)

    def attend(w):
        for i, peer in enumerate(group):
            from_j = [z * 0 + 2 * h + 1 - c, 2 * (1 - h) + c, 2 * (1 - h) + 1 - c][i]
            arrived(kvt.at[w, from_j], kv_s.at[w, i], kv_r.at[w, i], peer)
        kt = kvt[w, 0:2].reshape(HD, T)
        vt = kvt[w, 2:4].reshape(HD, T)
        visible = seqr_ref[...] <= seqc_ref[...]
        for i in range(2):
            cols = slice(i * HD, (i + 1) * HD)
            scores = jnp.where(visible, mm(qrot[:, cols], kt) * SCALE, NEG_FILL)
            raised = jnp.exp(scores - jnp.max(scores, axis=-1, keepdims=True))
            p = raised / jnp.sum(raised, axis=-1, keepdims=True)
            if w == 0:
                prob[i] = p
            else:
                att[:, cols] = mm_nt(p.astype(BF16), vt).astype(BF16)

    def grad_attended():
        whole(GRAD)
        accg[...] = jnp.zeros_like(accg)

        def body(x, at):
            accg[...] += mm_nt(x, wo[:, pl.ds(at, 1024)])

        each_chunk(GRAD, body)
        gab[...] = accg[...].astype(BF16)
        gatr[...] = accg[...].T.astype(BF16)

    def attention_back():
        kt = kvt[0, 0:2].reshape(HD, T)
        vt = kvt[0, 2:4].reshape(HD, T)
        key_sum = jnp.zeros((HD, T), F32)
        value_sum = jnp.zeros((HD, T), F32)
        for i in range(2):
            cols = slice(i * HD, (i + 1) * HD)
            p = prob[i]
            dp = mm(gab[:, cols], vt)
            sg = (p * (dp - jnp.sum(p * dp, axis=-1, keepdims=True)) * SCALE).astype(BF16)
            qg[:, cols] = rotate(mm_nt(sg, kt), cos_ref[...], -sin_ref[...]).astype(BF16)
            key_sum += mm(qtr[i], sg)
            value_sum += mm(gatr[cols, :], p.astype(BF16))
        kgs[0:2] = key_sum.reshape(2, 64, T).astype(BF16)
        kgs[2:4] = value_sum.reshape(2, 64, T).astype(BF16)
        for i, peer in enumerate(group):
            to_j = [2 * h + 1 - c, 2 * (1 - h) + c, 2 * (1 - h) + 1 - c][i]
            send(kgs.at[to_j], kgr.at[i], kg_s.at[i], kg_r.at[i], peer)

    def keyval_sum():
        total = kgs[j].astype(F32)
        for i, peer in enumerate(group):
            arrived(kgr.at[i], kg_s.at[i], kg_r.at[i], peer)
            total += kgr[i].astype(F32)
        total = jnp.concatenate([total, total], axis=0).T
        kvg[...] = rotate(total, kvcos_ref[...], -kvsin_ref[...]).astype(BF16)

    def spread(w, first):
        def chunk(k, _):
            at = pl.multiple_of(k * 256, 256)
            lows, highs = first(at), first(at + ENC // 2)
            for b in range(32):
                hh, zz, cc = b // 16, (b // 2) % 8, b % 2
                rows = slice(b * 8, b * 8 + 8)
                both = jnp.concatenate([lows[rows], highs[rows]], axis=0)
                rsb[w, cc, hh, zz, :, pl.ds(at, 256)] = both.astype(BF16)
            return 0

        lax.fori_loop(0, ENC // 512, chunk, 0)
        send(rsb.at[w, 1 - c], r1.at[w], rs_s.at[w, 0], rs_r.at[w, 0], sib)

    def fwd_part(at):
        return mm(att[...], woe[:, pl.ds(at, 256)])

    def back_part(at):
        return mm_nt(qg[...], qe[pl.ds(at, 256), :]) + mm_nt(kvg[:, :64], kve[pl.ds(at, 256), :])

    def reduce_x(w):
        arrived(r1.at[w], rs_s.at[w, 0], rs_r.at[w, 0], sib)
        rsb[w, c, 1 - h] = (rsb[w, c, 1 - h].astype(F32) + r1[w, 1 - h].astype(F32)).astype(BF16)
        send(rsb.at[w, c, 1 - h], r2.at[w], rs_s.at[w, 1], rs_r.at[w, 1], link["X"])

    def reduce_z(w):
        arrived(r2.at[w], rs_s.at[w, 1], rs_r.at[w, 1], link["X"])
        total = rsb[w, c, h].astype(F32) + r1[w, h].astype(F32) + r2[w].astype(F32)
        rsb[w, c, h] = total.astype(BF16)
        for k in range(1, 8):
            send(rsb.at[w, c, h, zmod(k)], r3.at[w, k - 1], rs_s.at[w, 1 + k], rs_r.at[w, 1 + k], along[k - 1])

    def reduced(w):
        total = rsb[w, c, h, z].astype(F32)
        for k in range(1, 8):
            arrived(r3.at[w, k - 1], rs_s.at[w, 1 + k], rs_r.at[w, 1 + k], along[k - 1])
            total += r3[w, k - 1].astype(F32)
        return total

    def decode_piece(encoded, i):
        rows, col = (i // 8) * 8, (i % 8) * 128
        return mm(encoded[rows : rows + 8, col : col + 128].astype(BF16), dec_bd[i * 128 : i * 128 + 128, :])

    def encode_piece(values, i):
        return mm(values, enc_bd[i * 512 : i * 512 + 512, :])

    def pass_on(w, make, out, peer):
        for i in range(8):
            both = []
            for q in (i, i + 8):
                value = make(q).astype(BF16)
                out[:, q * 512 : q * 512 + 512] = value
                both.append(encode_piece(value, q))
            pk_s[w, :, i * 128 : i * 128 + 128] = jnp.concatenate(both, axis=0).astype(BF16)
        send(pk_s.at[w], pk_r.at[w], sc_s.at[w], sc_r.at[w], peer)

    def received(w, out, peer, keep):
        arrived(pk_r.at[w], sc_s.at[w], sc_r.at[w], peer)
        got = pk_r[w].astype(F32)
        got = got * jnp.where(keep, 1.0, 0.0)
        for i in range(16):
            out[:, i * 512 : i * 512 + 512] = decode_piece(got, i).astype(BF16)

    def finish_forward():
        total = reduced(1)

        def make(i):
            return fwd_ref[:, i * 512 : i * 512 + 512].astype(F32) + decode_piece(total, i)

        pass_on(1, make, out_ref, nxt)

    def finish_back():
        total = reduced(0)
        dots = jnp.zeros((8, 1), F32)
        for i in range(16):
            cols = slice(i * 512, i * 512 + 512)
            scaled = decode_piece(total, i) * gain_ref[:, cols]
            scaled_ref[:, cols] = scaled
            dots += jnp.sum(scaled * saved_ref[:, cols].astype(F32), axis=-1, keepdims=True)
        factor = factor_ref[:, :1]
        pull = factor * factor * (dots * (1.0 / D))

        def make(i):
            cols = slice(i * 512, i * 512 + 512)
            x = saved_ref[:, cols].astype(F32)
            return grad_ref[:, cols].astype(F32) + factor * (scaled_ref[:, cols] - x * pull)

        pass_on(0, make, ig_ref, prv)

    def forward_tail():
        project(FWD, 1)
        reduce_z(0)
        attend(1)
        spread(1, fwd_part)
        reduce_x(1)
        finish_back()
        reduce_z(1)
        received(0, gs_ref, nxt, s < 7)
        finish_forward()
        received(1, act_ref, prv, s > 0)

    tasks = {
        "enc": make_enc,
        "woe": make_woe,
        "qe": make_qe,
        "projS": lambda: project(SAVED, 0),
        "attS": lambda: attend(0),
        "gatt": grad_attended,
        "bwd": attention_back,
        "kvsum": keyval_sum,
        "rsb0": lambda: spread(0, back_part),
        "rsb1": lambda: reduce_x(0),
        "fwd": forward_tail,
    }
    at = [0, 0, 0]
    for item in ORDER:
        if isinstance(item, str):
            tasks[item]()
        else:
            step(item, at[item])
            at[item] += 1
    assert at == [len(GROUPS)] * 3
    for copy in pending:
        copy.wait_send()


def on_device(
    fwd_in, saved_in, grad_in, norm_gain, query_weight, keyval_weight, out_weight, encoder, decoder, seq_pos, rope_ids
):
    def by_row(ids):
        return ids.reshape(8, 2, 16).transpose(1, 0, 2).reshape(T)

    t = lax.axis_index("tensor")
    rope = by_row(rope_ids).astype(F32)
    seq = by_row(seq_pos)
    pair_index = jnp.arange(HD // 2, dtype=F32)
    frequency = ROPE_BASE ** (-2.0 * pair_index / HD)
    angle = rope[:, None] * frequency[None, :]
    cosine, sine = jnp.cos(angle), jnp.sin(angle)
    cos_all = jnp.repeat(cosine, 2, axis=1)
    sin_all = jnp.stack([-sine, sine], axis=-1).reshape(T, HD)
    j = t % 4
    zeros = jnp.zeros((T, 64), F32)
    kv_cos = jnp.where(j == 0, cos_all[:, :64], jnp.where(j == 1, cos_all[:, 64:], 1.0))
    kv_sin = jnp.where(j == 0, sin_all[:, :64], jnp.where(j == 1, sin_all[:, 64:], 0.0))
    kv_cos = jnp.concatenate([kv_cos, zeros], axis=1)
    kv_sin = jnp.concatenate([kv_sin, zeros], axis=1)

    vmem = pl.BlockSpec(memory_space=pltpu.VMEM)
    hbm = pl.BlockSpec(memory_space=pl.ANY)
    dma = pltpu.SemaphoreType.DMA
    outs = pl.pallas_call(
        kernel,
        out_shape=[jax.ShapeDtypeStruct((8, D), BF16)] * 4,
        in_specs=[vmem] * 10 + [hbm] * 5,
        out_specs=[vmem] * 4,
        scratch_shapes=[
            pltpu.VMEM((3, 2, 16, 16, HALF), BF16),
            pltpu.VMEM((D, 256), BF16),
            pltpu.VMEM((D, 64), BF16),
            pltpu.VMEM((256, D), BF16),
            pltpu.VMEM((D, 32), F32),
            pltpu.VMEM((ENC, 128), F32),
            pltpu.VMEM((D, 128), BF16),
            pltpu.VMEM((ENC, 512), BF16),
            pltpu.VMEM((ENC, 512), BF16),
            pltpu.VMEM((256, ENC), BF16),
            pltpu.VMEM((ENC, 256), BF16),
            pltpu.VMEM((ENC, 64), BF16),
            pltpu.VMEM((3, 2, 8, HALF), F32),
            pltpu.VMEM((3, 2, 8, HALF), F32),
            pltpu.VMEM((8, 128), F32),
            pltpu.VMEM((T, 256), F32),
            pltpu.VMEM((T, 128), F32),
            pltpu.VMEM((T, 256), F32),
            pltpu.VMEM((2, 4, 64, T), BF16),
            pltpu.VMEM((T, 256), BF16),
            pltpu.VMEM((2, HD, T), BF16),
            pltpu.VMEM((T, 256), BF16),
            pltpu.VMEM((256, T), BF16),
            pltpu.VMEM((2, T, T), F32),
            pltpu.VMEM((T, 256), BF16),
            pltpu.VMEM((T, 256), BF16),
            pltpu.VMEM((T, 128), BF16),
            pltpu.VMEM((4, 64, T), BF16),
            pltpu.VMEM((3, 64, T), BF16),
            pltpu.VMEM((2, 2, 2, 8, 16, ENC // 2), BF16),
            pltpu.VMEM((2, 2, 8, 16, ENC // 2), BF16),
            pltpu.VMEM((2, 8, 16, ENC // 2), BF16),
            pltpu.VMEM((2, 7, 16, ENC // 2), BF16),
            pltpu.VMEM((2, 16, ENC // 2), BF16),
            pltpu.VMEM((2, 16, ENC // 2), BF16),
            pltpu.VMEM((8, D), F32),
            dma((5,)),
            dma((3,)),
            dma((3,)),
            dma((3, len(KEYS))),
            dma((3, len(KEYS))),
            dma((3, len(BLOCKS))),
            dma((3, len(BLOCKS))),
            dma((2, 3)),
            dma((2, 3)),
            dma((3,)),
            dma((3,)),
            dma((2, 9)),
            dma((2, 9)),
            dma((2,)),
            dma((2,)),
        ],
        compiler_params=pltpu.CompilerParams(collective_id=0, has_side_effects=True, vmem_limit_bytes=60 << 20),
        name="relay_tick",
    )(
        fwd_in[0],
        saved_in[0],
        grad_in[0],
        norm_gain,
        cos_all,
        sin_all,
        kv_cos,
        kv_sin,
        seq[:, None],
        seq[None, :],
        query_weight[0],
        keyval_weight[0],
        out_weight[0],
        encoder.reshape(D, 32),
        decoder.reshape(ENC, 128),
    )
    return tuple(o[None] for o in outs)


def solution(mesh):
    rows = P("section", "tensor", None)
    columns = P("section", None, "tensor")
    return jax.shard_map(
        on_device,
        mesh=mesh,
        in_specs=(rows, rows, rows, P("section", None), columns, columns, rows, P(), P(), P(), P()),
        out_specs=(rows, rows, rows, rows),
        check_vma=False,
    )
```

time: 564 us -> 135 us (0.24); the launches traced: 557 us -> 135 us
  waiting for transfers between devices: 432 us -> 0 us
  Pallas kernels: 0 us -> 118 us
  matrix products: 64 us -> 0 us
  starting transfers between devices: 16.8 us -> 0 us
  between operations: 14.7 us -> 0.8 us
  local copies, waits for them, and re-layouts: 22.6 us -> 14.9 us
  other arithmetic: 7.25 us -> 1.56 us
    all_gather x3 -> x0, waiting for transfers between devices: 221 us -> none  [the longest x2 154 us: forward_parts(): lax.all_gather(normed, 'tensor', axis=0, tiled=True)]
    reduce_scatter x2 -> x0, waiting for transfers between devices: 202 us -> none  [reduce_rows(): lax.psum_scatter(encoded.astype(jnp.bfloat16), 'tensor', scatter_dimensio...]
    pallas_call x0 -> x1, Pallas kernels: none -> 118 us  [on_device(): pl.pallas_call(kernel, out_shape=[jax.ShapeDtypeStruct((8, D), BF16)] * 4...]
    dot_general x22 -> x0, matrix products: 62.6 us -> none  [the longest x4 18.9 us: encode_blocks(): jnp.einsum('tbi,bio->tbo', grouped, encoder, precision=lax.Precision.HIGH...]
    ppermute x8 -> x0, starting transfers between devices: 16.6 us -> none  [the longest x2 9.18 us: passed_along(): return lax.ppermute(x, axis, pairs)]
    dot_general x3 -> x0, local copies, waits for them, and re-layouts: 15.8 us -> none  [the longest x2 14.1 us: project_rows(): jnp.dot(row_piece, query_matrix, preferred_element_type=jnp.float32)]
    unnamed x20 -> x14, local copies, waits for them, and re-layouts: 0.06 us -> 10.7 us
    ppermute x8 -> x0, waiting for transfers between devices: 8.18 us -> none  [the longest x2 5.07 us: passed_along(): return lax.ppermute(x, axis, pairs)]
  transfers between devices with their start and end apart: 13 -> 0, of which waited for: 9 -> 0; matrix products, arithmetic and copies ran while one was open for 14% -> 0% of each run, Pallas kernels for 0% -> 0%
where the time goes in v1:
time: 135 us
  Pallas kernels  118 us (87%)
  local copies, waits for them, and re-layouts  14.9 us (11%)
  other arithmetic  1.56 us (1%)
    pallas_call x1, Pallas kernels, on_device(): pl.pallas_call(kernel, out_shape=[jax.ShapeDtypeStruct((8, D), BF16)] * 4...  118 us
    unnamed x14, local copies, waits for them, and re-layouts  10.7 us

profile of v1, /device:TPU:2, one launch (start us, length us, event | category | flops | bytes accessed | tf_op | source)
XLA Modules:
  0.0 134.9 jit_solution(8736033375412493)
XLA Ops:
  0.6 0.0 copy-start.3
  0.6 0.0 copy-start.2
  0.7 0.8 convert_element_type.16
  1.5 0.1 convert_element_type.17
  1.6 0.1 convert_element_type.19
  1.7 0.8 reshape.128
  2.5 0.7 broadcast_in_dim_reshape.7.seqr_ref
  3.1 0.3 multiply_cosine_fusion
  3.5 0.1 reshape.126
  3.6 0.1 copy.50.cos_ref
  3.7 0.0 copy-start
  3.7 0.8 broadcast_in_dim_reshape.8.seqc_ref
  4.5 0.3 fusion.2
  4.8 0.1 copy.41
  4.9 0.1 reshape.127
  5.0 0.1 copy.51.sin_ref
  5.1 0.0 copy-start.1
  5.1 0.1 fusion
  5.2 0.7 concatenate.7.kvsin_ref
  5.9 0.7 concatenate.6.kvcos_ref
  6.6 0.0 copy-done.2
  6.6 1.8 %copy.48 = bf16[1,8192,64]{2,1,0:T(8,128)(2,1)} copy(bf16[1,8192,64]{1,2,0:T(8,128)(2,1)S(1)} %copy-done.2) | data formatting | bytes 2097152 | tf_op args[5]
  8.4 0.0 copy-done.3
  8.4 2.6 %copy.49 = f32[64,128,32]{2,1,0:T(8,128)} copy(f32[64,128,32]{1,2,0:T(8,128)S(1)} %copy-done.3) | data formatting | bytes 2097152 | tf_op args[7]
  11.0 0.0 copy-done
  11.0 0.0 copy-done.1
  11.0 117.6 %relay_tick.1 = (bf16[8,8192]{1,0:T(8,128)(2,1)}, bf16[8,8192]{1,0:T(8,128)(2,1)}, bf16[8,8192]{1,0:T(8,128)(2,1)}, bf16[8,8192]{1,0:T(8,128)(2,1)}) custom-call(bf16[8,8192]{1,0:T(8,128)(2,1)} %bitcast.23, bf16[8,8192]{1,0:T(8,128)(2,1)} %bitcast.24, bf16[8,8192]{1,0:T(8,128)(2,1)} %bitcast.25, f32[1,8192]{1,0:T(1,128)} %gain_ref.1, f32[256,128]{1,0:T(8,128)} %copy-done, ...), custom_call_target="tpu_custom_call" | custom-call | tf_op jit(solution)/shard_map/relay_tick/pallas_call | solution.py:456
  128.6 1.6 %copy.57 = bf16[1,8,8192]{2,1,0:T(8,128)(2,1)} copy(bf16[1,8,8192]{2,1,0:T(8,128)(2,1)} %bitcast.29) | data formatting | bytes 262144
  130.2 1.6 %copy.58 = bf16[1,8,8192]{2,1,0:T(8,128)(2,1)} copy(bf16[1,8,8192]{2,1,0:T(8,128)(2,1)} %bitcast.28) | data formatting | bytes 262144
  131.7 1.6 %copy.59 = bf16[1,8,8192]{2,1,0:T(8,128)(2,1)} copy(bf16[1,8,8192]{2,1,0:T(8,128)(2,1)} %bitcast.27) | data formatting | bytes 262144
  133.3 1.6 %copy.60 = bf16[1,8,8192]{2,1,0:T(8,128)(2,1)} copy(bf16[1,8,8192]{2,1,0:T(8,128)(2,1)} %bitcast.26) | data formatting | bytes 262144
  (5 shorter events, 0.1 us)
Async XLA Ops:
  0.6 7.7 %copy-start.3 = (f32[64,128,32]{1,2,0:T(8,128)S(1)}, f32[64,128,32]{1,2,0:T(8,128)}, u32[]{:S(2)}) copy-start(f32[64,128,32]{1,2,0:T(8,128)} %param.18) | copy-start | bytes 3145732
  0.6 5.9 %copy-start.2 = (bf16[1,8192,64]{1,2,0:T(8,128)(2,1)S(1)}, bf16[1,8192,64]{1,2,0:T(8,128)(2,1)}, u32[]{:S(2)}) copy-start(bf16[1,8192,64]{1,2,0:T(8,128)(2,1)} %param.16) | copy-start | bytes 3145732
  3.7 7.3 %copy-start = (f32[256,128]{1,0:T(8,128)}, f32[256,128]{1,0:T(8,128)S(1)}, u32[]{:S(2)}) copy-start(f32[256,128]{1,0:T(8,128)S(1)} %copy.50.cos_ref) | copy-start | bytes 393220
  5.1 5.9 %copy-start.1 = (f32[256,128]{1,0:T(8,128)}, f32[256,128]{1,0:T(8,128)S(1)}, u32[]{:S(2)}) copy-start(f32[256,128]{1,0:T(8,128)S(1)} %copy.51.sin_ref) | copy-start | bytes 393220

commit v2 on v1

v2 whole, which is shorter than its diff:
```python
import math

import jax
import jax.numpy as jnp
import numpy as np
from jax import lax
from jax.experimental import pallas as pl
from jax.experimental.pallas import tpu as pltpu
from jax.sharding import PartitionSpec as P

MESH = pl.DeviceIdType.MESH
HD = 128
D = 8192
HALF = D // 2
ENC = 2048
T = 256
EPSILON = 1e-05
ROPE_BASE = 10000.0
NEG_FILL = -1e30
SCALE = 1.0 / math.sqrt(HD)
F32 = jnp.float32
BF16 = jnp.bfloat16
GRAD, SAVED, FWD = 0, 1, 2

KEYS = [(0, 1), (0, -1), (0, 2), (0, -2), (0, 3), (0, -3), (0, 4, 0), (0, 4, 1)]
KEYS += [(1, 0), (1, 1), (1, -1), (1, 2), (1, -2), (1, 3), (1, -3), (1, 4, 0), (1, 4, 1)]
COLUMNS = [[k for k in KEYS if k[0] == 0], [k for k in KEYS if k[0] == 1]]
ORDER = [
    ("S", 0, "M", (0, 0)), ("S", 0, "P", (0, 0)), ("S", 0, "X", (0, 0)), "tables", ("S", 1, "M", (0, 0)),
    ("S", 1, "P", (0, 0)), ("S", 1, "X", (0, 0)), "enc", ("W", 0, (0, 1)), ("S", 0, "M", (0, 1)),
    ("W", 0, (0, -1)), ("S", 0, "P", (0, -1)), ("S", 0, "X", (0, 1)), ("S", 0, "X", (0, -1)),
    ("S", 2, "M", (0, 0)), ("S", 2, "P", (0, 0)), ("S", 2, "X", (0, 0)), "woe0", "woe1", ("W", 1, (0, 1)),
    ("S", 1, "M", (0, 1)), ("W", 1, (0, -1)), ("S", 1, "P", (0, -1)), ("S", 1, "X", (0, 1)), "woe2", "woe3", "qe0",
    ("W", 0, (0, 2)), ("S", 0, "M", (0, 2)), ("W", 0, (0, -2)), ("S", 0, "P", (0, -2)), ("S", 0, "X", (0, 2)),
    ("S", 0, "X", (0, -2)), "qe1", "qe2", ("W", 2, (0, 1)), ("S", 2, "M", (0, 1)), ("W", 2, (0, -1)),
    ("S", 2, "P", (0, -1)), "qe3", ("W", 1, (0, 2)), ("S", 1, "M", (0, 2)), ("W", 1, (0, -2)),
    ("S", 1, "P", (0, -2)), ("S", 1, "X", (0, 2)), ("S", 1, "X", (0, -2)), ("W", 0, (0, 3)), ("S", 0, "M", (0, 3)),
    ("W", 0, (0, -3)), ("S", 0, "P", (0, -3)), ("W", 2, (0, 2)), ("S", 2, "M", (0, 2)), ("S", 1, "X", (0, -1)),
    ("W", 0, (1, 2)), ("S", 0, "M", (1, 2)), ("W", 2, (0, -2)), ("S", 2, "P", (0, -2)), ("S", 2, "X", (0, 2)),
    ("W", 1, (0, 3)), ("S", 1, "M", (0, 3)), ("W", 1, (0, -3)), ("S", 1, "P", (0, -3)), ("W", 0, (1, -2)),
    ("S", 0, "P", (1, -2)), ("S", 2, "X", (0, -2)), ("W", 0, (0, 4, 0)), ("W", 0, (0, 4, 1)), "g00", "g01", "g02",
    ("W", 1, (1, 2)), ("S", 1, "M", (1, 2)), "g03", "gx0", ("W", 2, (0, 3)), ("S", 2, "M", (0, 3)),
    ("W", 2, (0, -3)), ("S", 2, "P", (0, -3)), ("S", 2, "X", (0, 1)), ("W", 1, (1, -2)), ("S", 1, "P", (1, -2)),
    ("W", 0, (1, 3)), ("S", 0, "M", (1, 3)), ("W", 1, (0, 4, 0)), ("W", 1, (0, 4, 1)), "s00", ("W", 0, (1, -3)),
    ("S", 0, "P", (1, -3)), ("S", 2, "X", (0, -1)), "s01", "s02", "s03", "sx0", ("W", 1, (1, 3)),
    ("S", 1, "M", (1, 3)), ("W", 2, (1, 2)), ("S", 2, "M", (1, 2)), ("W", 2, (0, 4, 0)), ("W", 2, (0, 4, 1)),
    "f00", ("W", 1, (1, -3)), ("S", 1, "P", (1, -3)), "f01", "f02", ("W", 2, (1, -2)), ("S", 2, "P", (1, -2)),
    ("W", 0, (1, 0)), ("W", 0, (1, 1)), ("W", 0, (1, -1)), ("W", 0, (1, 4, 0)), ("W", 0, (1, 4, 1)), "g10", "g11",
    "g12", "g13", "gx1", ("W", 1, (1, 0)), ("W", 1, (1, 1)), ("W", 1, (1, -1)), ("W", 1, (1, 4, 0)),
    ("W", 1, (1, 4, 1)), "s10", "s11", ("W", 2, (1, 3)), ("S", 2, "M", (1, 3)), "s12", "s13", ("W", 2, (1, -3)),
    ("S", 2, "P", (1, -3)), "sx1", "f03", "fx0", "gfin", "sfin", ("W", 2, (1, 0)), ("W", 2, (1, 1)),
    ("W", 2, (1, -1)), ("W", 2, (1, 4, 0)), ("W", 2, (1, 4, 1)), "f10", "f11", "f12", "f13", "fx1", "attS", "bwd",
    "ffin", "kvsum", "sp00", "sp01", "attF", "rx00", "rx01", "sp10", "sp11", "rx10", "rz00", "rx11", "rz01",
    "rz10", "rz11", "fin0", "fin1", "rcv0", "rcv1",
]


def mm(a, b):
    return jnp.dot(a, b, preferred_element_type=F32)


def mm_nt(a, b):
    return lax.dot_general(a, b, (((1,), (1,)), ((), ())), preferred_element_type=F32)


def rotate(x, cosine, sine):
    lane = lax.broadcasted_iota(jnp.int32, x.shape, 1)
    swapped = jnp.where(lane % 2 == 0, pltpu.roll(x, x.shape[1] - 1, 1), pltpu.roll(x, 1, 1))
    return x * cosine + swapped * sine


def kernel(
    fwd_hbm, saved_hbm, grad_hbm, gain_hbm, freq_hbm, rope_hbm, seq_hbm, wq_hbm, wkv_hbm, wo_hbm, enc_hbm, dec_hbm,
    out_hbm, act_hbm, ig_hbm, gs_hbm,
    fwd_ref, saved_ref, grad_ref, gain_ref, freq_ref, rope_ref, seq_ref, wq, wkv, wo, enc_raw, dec_raw, wqs, wkvp, wos,
    out_ref, act_ref, ig_ref, gs_ref,
    G, cos_ref, sin_ref, kvcos_ref, kvsin_ref, seqc_ref, seqr_ref, enc_bd, enc_t, dec_bd, woe, qe, kve,
    nrm, chipf, factor_ref, acc, acckv, other, got, gotkv, kvt, qrot, qtr, gab, gatr, prob, att, qg, kvg, kgs, kgr,
    rsb, r1, r2, r3, pk_s, pk_r, scaled_ref,
    wsem, osem, ws_s, ws_r, st_s, st_r, g_s, g_r, sb_s, sb_r, kv_s, kv_r, kg_s, kg_r, rs_s, rs_r, sc_s, sc_r,
):
    s = lax.axis_index("section")
    t = lax.axis_index("tensor")
    z, h, c = t // 4, (t // 2) % 2, t % 2
    j = t % 4

    def tid(zz, hh, cc):
        return (s, zz * 4 + hh * 2 + cc)

    def zmod(d):
        return lax.rem(z + d + 8, 8)

    sib = tid(z, h, 1 - c)
    link = {"M": tid(zmod(-1), h, c), "P": tid(zmod(1), h, c), "X": tid(z, 1 - h, c)}
    group = [sib, link["X"], tid(z, 1 - h, 1 - c)]
    nxt, prv = (lax.rem(s + 1, 8), t), (lax.rem(s + 7, 8), t)
    along = [tid(zmod(k), h, c) for k in range(1, 8)]

    arrays = {
        "grad": (grad_hbm, grad_ref), "saved": (saved_hbm, saved_ref), "gain": (gain_hbm, gain_ref), "fwd": (fwd_hbm, fwd_ref),
        "rope": (rope_hbm, rope_ref), "seq": (seq_hbm, seq_ref), "freq": (freq_hbm, freq_ref),
        "enc": (enc_hbm, enc_raw), "dec": (dec_hbm, dec_raw), "wo": (wo_hbm, wo), "wq": (wq_hbm, wq), "wkv": (wkv_hbm, wkv),
        "own": (wkv_hbm.at[:, pl.ds(pl.multiple_of(c * HALF, HALF), HALF)], wkvp.at[:64]),
    }
    loads = {}
    for i, (name, (src, dst)) in enumerate(arrays.items()):
        loads[name] = pltpu.make_async_copy(src, dst, wsem.at[i])
        loads[name].start()

    barrier = pltpu.get_barrier_semaphore()
    for peer in along + group + [nxt, prv]:
        pl.semaphore_signal(barrier, inc=1, device_id=peer, device_id_type=MESH)

    def put_own(a, values):
        nrm[a, 0] = values[:, :HALF]
        nrm[a, 1] = values[:, HALF:]

    def normed(ref, slot):
        x = ref[...].astype(F32)
        factor = lax.rsqrt(jnp.mean(x * x, axis=-1, keepdims=True) + EPSILON)
        if slot is not None:
            factor_ref[...] = jnp.broadcast_to(factor, factor_ref.shape)
        return x * factor * gain_ref[...]

    pending, stores = [], []

    def store(i, src, dst):
        stores.append(pltpu.make_async_copy(src, dst, osem.at[i]))
        stores[-1].start()

    def send(src, dst, ssem, rsem, peer):
        copy = pltpu.make_async_remote_copy(
            src_ref=src, dst_ref=dst, send_sem=ssem, recv_sem=rsem, device_id=peer, device_id_type=MESH
        )
        copy.start()
        pending.append(copy)

    def arrived(dst, ssem, rsem, peer):
        pltpu.make_async_remote_copy(
            src_ref=dst, dst_ref=dst, send_sem=ssem, recv_sem=rsem, device_id=peer, device_id_type=MESH
        ).wait_recv()

    def stage(a):
        send(nrm.at[a, 1 - c], chipf.at[a, c], st_s.at[a], st_r.at[a], sib)

    loads["grad"].wait()
    put_own(GRAD, grad_ref[...].astype(F32))
    pl.semaphore_wait(barrier, len(along) + len(group) + 2)
    stage(GRAD)
    loads["saved"].wait()
    loads["gain"].wait()
    put_own(SAVED, normed(saved_ref, 0))
    stage(SAVED)

    away = pl.ds(pl.multiple_of((1 - c) * HALF, HALF), HALF)
    shared = [(wo_hbm.at[:, away], wos), (wkv_hbm.at[:, away], wkvp.at[64:]), (wq_hbm.at[away, :], wqs)]
    for i, (src, dst) in enumerate(shared):
        send(src, dst, ws_s.at[i], ws_r.at[i], sib)

    def shared_in(i):
        arrived(shared[i][1], ws_s.at[i], ws_r.at[i], sib)

    def stage_last():
        loads["fwd"].wait()
        put_own(FWD, normed(fwd_ref, None))
        stage(FWD)

    def make_tables():
        loads["rope"].wait()
        loads["seq"].wait()
        loads["freq"].wait()

        def down(row):
            tall = jnp.broadcast_to(row.astype(F32), (128, T)).T
            return jnp.concatenate([tall[zz * 32 + hh * 16 :][:16] for hh in range(2) for zz in range(8)], axis=0)

        positions = down(seq_ref[...])
        seqc_ref[...] = positions
        seqr_ref[...] = positions.T[:8]
        angle = down(rope_ref[...]) * freq_ref[...]
        cosine, sine = jnp.cos(angle), jnp.sin(angle)
        sine = jnp.where(lax.broadcasted_iota(jnp.int32, sine.shape, 1) % 2 == 0, -sine, sine)
        cos_ref[...] = cosine
        sin_ref[...] = sine
        first, second = jnp.where(j == 0, 1.0, 0.0), jnp.where(j == 1, 1.0, 0.0)
        kvcos_ref[...] = first * cosine + second * pltpu.roll(cosine, 64, 1) + (1.0 - first - second)
        kvsin_ref[...] = first * sine + second * pltpu.roll(sine, 64, 1)

    def where(key):
        return (h if key[0] == 0 else 1 - h), zmod(key[1])

    def piece(a, key):
        ref = G.at[(a, *where(key))]
        if len(key) == 3:
            ref = ref.at[:, pl.ds(key[2] * (HALF // 2), HALF // 2)]
        return ref

    def form_own(a):
        if a == FWD:
            stage_last()
        arrived(chipf.at[a, 1 - c], st_s.at[a], st_r.at[a], sib)
        chipf[a, c] = nrm[a, c]
        G[a, h, z] = chipf[a].reshape(16, HALF).astype(BF16)

    def take(a, key):
        i = KEYS.index(key)
        arrived(piece(a, key), g_s.at[a, i], g_r.at[a, i], link["M"])

    def hand(a, way, key):
        column, far = (key[0], key[1] + (1 if way == "M" else -1)) if way != "X" else (1 - key[0], key[1])
        there = (column, 4, 0 if way == "M" else 1) if abs(far) == 4 else (column, far)
        i = KEYS.index(there)
        part = piece(a, key + there[2:])
        send(part, part, g_s.at[a, i], g_r.at[a, i], link[way])

    def make_enc():
        loads["enc"].wait()
        loads["dec"].wait()

        def fill(i, _):
            rows = pl.ds(i * 128, 128)
            group_row = lax.broadcasted_iota(jnp.int32, (128, 128), 0) // 32
            e, d = enc_raw[rows, :], dec_raw[rows, :]
            wide = jnp.concatenate([jnp.where(group_row == q, e, 0.0) for q in range(4)], axis=1)
            enc_t[rows, :] = wide.astype(BF16)
            enc_bd[pl.ds(i * 512, 512), :] = wide.T.astype(BF16)
            wide = jnp.concatenate([jnp.where(group_row == q, d, 0.0) for q in range(4)], axis=1)
            dec_bd[rows, :] = wide.astype(BF16)
            return 0

        lax.fori_loop(0, 16, fill, 0)

    def make_woe(part):
        if part == 0:
            loads["wo"].wait()

        def fill(i, _):
            cols = pl.ds(pl.multiple_of(i * 512, 512), 512)
            outs = pl.ds(pl.multiple_of(i * 128, 128), 128)
            woe[:, outs] = mm(wo[:, cols], enc_bd[pl.ds(i * 512, 512), :]).astype(BF16)
            return 0

        lax.fori_loop(part * 4, part * 4 + 4, fill, 0)

    def make_qe(part):
        if part == 0:
            loads["wq"].wait()
            loads["wkv"].wait()

        def fill(i, _):
            rows, outs = pl.ds(i * 512, 512), pl.ds(i * 128, 128)
            e = enc_t[outs, :]
            qe[outs, :] = mm(e, wq[rows, :]).astype(BF16)
            kve[outs, :] = mm_nt(e, wkv[:, pl.ds(pl.multiple_of(i * 512, 512), 512)]).astype(BF16)
            return 0

        lax.fori_loop(part * 4, part * 4 + 4, fill, 0)

    def rows_of(part):
        return pl.ds(pl.multiple_of((h if part == 0 else 1 - h) * 128, 128), 128)

    def contract(a, part, k):
        if part == 0 and k == 0:
            for i in [0] if a == GRAD else [1, 2]:
                if a != FWD:
                    shared_in(i)
            if a == SAVED:
                loads["own"].wait()
        rows, cols = rows_of(part), slice(k * 1024, k * 1024 + 1024)
        here = pl.ds(pl.multiple_of(c * HALF + k * 1024, 1024), 1024)
        x = G[a, h if part == 0 else 1 - h, :, :, cols].reshape(128, 1024)
        if a == GRAD:
            products = [(acc, mm_nt(x, wo[:, here])), (other, mm_nt(x, wos[:, cols]))]
        else:
            products = [(acc, mm(x, wq[here, :])), (other, mm(x, wqs[cols, :])), (acckv, mm_nt(x, wkvp[:, cols]))]
        for ref, product in products:
            if k == 0:
                ref[a, rows, :] = product
            else:
                ref[a, rows, :] += product

    def swap(a, part):
        rows = rows_of(part)
        send(other.at[a, rows], got.at[a, rows], sb_s.at[a, part, 0], sb_r.at[a, part, 0], sib)
        if a != GRAD:
            send(acckv.at[a, rows], gotkv.at[a, rows], sb_s.at[a, part, 1], sb_r.at[a, part, 1], sib)

    def swapped(a):
        for part in range(2):
            rows = rows_of(part)
            arrived(got.at[a, rows], sb_s.at[a, part, 0], sb_r.at[a, part, 0], sib)
            if a != GRAD:
                arrived(gotkv.at[a, rows], sb_s.at[a, part, 1], sb_r.at[a, part, 1], sib)

    def project(a, w):
        swapped(a)
        keyval = acckv[a] + pltpu.roll(gotkv[a], 64, 1)
        turned = rotate(keyval, kvcos_ref[...], kvsin_ref[...])
        kvt[w, j] = turned.T[:64].astype(BF16)
        for i, peer in enumerate(group):
            send(kvt.at[w, j], kvt.at[w, j], kv_s.at[w, i], kv_r.at[w, i], peer)
        for i in range(2):
            cols = slice(i * HD, (i + 1) * HD)
            q = rotate(acc[a, :, cols] + got[a, :, cols], cos_ref[...], sin_ref[...])
            qrot[w, :, cols] = q.astype(BF16)
            if w == 0:
                qtr[i] = q.T.astype(BF16)

    def attend(w):
        for i, peer in enumerate(group):
            from_j = [z * 0 + 2 * h + 1 - c, 2 * (1 - h) + c, 2 * (1 - h) + 1 - c][i]
            arrived(kvt.at[w, from_j], kv_s.at[w, i], kv_r.at[w, i], peer)
        kt = kvt[w, 0:2].reshape(HD, T)
        vt = kvt[w, 2:4].reshape(HD, T)
        visible = seqr_ref[:1, :] <= seqc_ref[:, :1]
        for i in range(2):
            cols = slice(i * HD, (i + 1) * HD)
            scores = jnp.where(visible, mm(qrot[w, :, cols], kt) * SCALE, NEG_FILL)
            raised = jnp.exp(scores - jnp.max(scores, axis=-1, keepdims=True))
            p = raised / jnp.sum(raised, axis=-1, keepdims=True)
            if w == 0:
                prob[i] = p
            else:
                att[:, cols] = mm_nt(p.astype(BF16), vt).astype(BF16)

    def grad_attended():
        swapped(GRAD)
        total = acc[GRAD] + got[GRAD]
        gab[...] = total.astype(BF16)
        gatr[...] = total.T.astype(BF16)

    def attention_back():
        kt = kvt[0, 0:2].reshape(HD, T)
        vt = kvt[0, 2:4].reshape(HD, T)
        key_sum = jnp.zeros((HD, T), F32)
        value_sum = jnp.zeros((HD, T), F32)
        for i in range(2):
            cols = slice(i * HD, (i + 1) * HD)
            p = prob[i]
            dp = mm(gab[:, cols], vt)
            sg = (p * (dp - jnp.sum(p * dp, axis=-1, keepdims=True)) * SCALE).astype(BF16)
            qg[:, cols] = rotate(mm_nt(sg, kt), cos_ref[...], -sin_ref[...]).astype(BF16)
            key_sum += mm(qtr[i], sg)
            value_sum += mm(gatr[cols, :], p.astype(BF16))
        kgs[0:2] = key_sum.reshape(2, 64, T).astype(BF16)
        kgs[2:4] = value_sum.reshape(2, 64, T).astype(BF16)
        for i, peer in enumerate(group):
            to_j = [2 * h + 1 - c, 2 * (1 - h) + c, 2 * (1 - h) + 1 - c][i]
            send(kgs.at[to_j], kgr.at[i], kg_s.at[i], kg_r.at[i], peer)

    def keyval_sum():
        total = kgs[j].astype(F32)
        for i, peer in enumerate(group):
            arrived(kgr.at[i], kg_s.at[i], kg_r.at[i], peer)
            total += kgr[i].astype(F32)
        total = jnp.concatenate([total, total], axis=0).T
        kvg[...] = rotate(total, kvcos_ref[...], -kvsin_ref[...]).astype(BF16)

    def spread(w, q, first):
        def chunk(k, _):
            at = pl.multiple_of(q * 512 + k * 256, 256)
            lows, highs = first(at), first(at + ENC // 2)
            for b in range(32):
                hh, zz, cc = b // 16, (b // 2) % 8, b % 2
                rows = slice(b * 8, b * 8 + 8)
                both = jnp.concatenate([lows[rows], highs[rows]], axis=0)
                rsb[w, q, cc, hh, zz, :, pl.ds(pl.multiple_of(k * 256, 256), 256)] = both.astype(BF16)
            return 0

        lax.fori_loop(0, 2, chunk, 0)
        send(rsb.at[w, q, 1 - c], r1.at[w, q], rs_s.at[w, q, 0], rs_r.at[w, q, 0], sib)

    def fwd_part(at):
        return mm(att[...], woe[:, pl.ds(at, 256)])

    def back_part(at):
        return mm_nt(qg[...], qe[pl.ds(at, 256), :]) + mm_nt(kvg[:, :64], kve[pl.ds(at, 256), :])

    def reduce_x(w, q):
        arrived(r1.at[w, q], rs_s.at[w, q, 0], rs_r.at[w, q, 0], sib)
        rsb[w, q, c, 1 - h] = (rsb[w, q, c, 1 - h].astype(F32) + r1[w, q, 1 - h].astype(F32)).astype(BF16)
        send(rsb.at[w, q, c, 1 - h], r2.at[w, q], rs_s.at[w, q, 1], rs_r.at[w, q, 1], link["X"])

    def reduce_z(w, q):
        arrived(r2.at[w, q], rs_s.at[w, q, 1], rs_r.at[w, q, 1], link["X"])
        total = rsb[w, q, c, h].astype(F32) + r1[w, q, h].astype(F32) + r2[w, q].astype(F32)
        rsb[w, q, c, h] = total.astype(BF16)
        for k in range(1, 8):
            sems = rs_s.at[w, q, 1 + k], rs_r.at[w, q, 1 + k]
            send(rsb.at[w, q, c, h, zmod(k)], r3.at[w, q, k - 1], *sems, along[k - 1])

    def reduced(w):
        totals = []
        for q in range(2):
            total = rsb[w, q, c, h, z].astype(F32)
            for k in range(1, 8):
                arrived(r3.at[w, q, k - 1], rs_s.at[w, q, 1 + k], rs_r.at[w, q, 1 + k], along[k - 1])
                total += r3[w, q, k - 1].astype(F32)
            totals.append(total)
        return jnp.concatenate(totals, axis=1)

    def decode_piece(encoded, i):
        rows, col = (i // 8) * 8, (i % 8) * 128
        return mm(encoded[rows : rows + 8, col : col + 128].astype(BF16), dec_bd[i * 128 : i * 128 + 128, :])

    def encode_piece(values, i):
        return mm(values, enc_bd[i * 512 : i * 512 + 512, :])

    def pass_on(w, make, out, peer):
        for i in range(8):
            both = []
            for q in (i, i + 8):
                value = make(q).astype(BF16)
                out[:, q * 512 : q * 512 + 512] = value
                both.append(encode_piece(value, q))
            pk_s[w, :, i * 128 : i * 128 + 128] = jnp.concatenate(both, axis=0).astype(BF16)
        send(pk_s.at[w], pk_r.at[w], sc_s.at[w], sc_r.at[w], peer)

    def received(w, out, peer, keep):
        arrived(pk_r.at[w], sc_s.at[w], sc_r.at[w], peer)
        got = pk_r[w].astype(F32)
        got = got * jnp.where(keep, 1.0, 0.0)
        for i in range(16):
            out[:, i * 512 : i * 512 + 512] = decode_piece(got, i).astype(BF16)

    def finish_forward():
        total = reduced(1)

        def make(i):
            return fwd_ref[:, i * 512 : i * 512 + 512].astype(F32) + decode_piece(total, i)

        pass_on(1, make, out_ref, nxt)
        store(0, out_ref, out_hbm)

    def finish_back():
        total = reduced(0)
        dots = jnp.zeros((8, 1), F32)
        for i in range(16):
            cols = slice(i * 512, i * 512 + 512)
            scaled = decode_piece(total, i) * gain_ref[:, cols]
            scaled_ref[:, cols] = scaled
            dots += jnp.sum(scaled * saved_ref[:, cols].astype(F32), axis=-1, keepdims=True)
        factor = factor_ref[:, :1]
        pull = factor * factor * (dots * (1.0 / D))

        def make(i):
            cols = slice(i * 512, i * 512 + 512)
            x = saved_ref[:, cols].astype(F32)
            return grad_ref[:, cols].astype(F32) + factor * (scaled_ref[:, cols] - x * pull)

        pass_on(0, make, ig_ref, prv)
        store(2, ig_ref, ig_hbm)

    def get_grad():
        received(0, gs_ref, nxt, s < 7)
        store(3, gs_ref, gs_hbm)

    def get_act():
        received(1, act_ref, prv, s > 0)
        store(1, act_ref, act_hbm)

    tasks = {
        "tables": make_tables,
        "enc": make_enc,
        "sfin": lambda: project(SAVED, 0),
        "attS": lambda: attend(0),
        "gfin": grad_attended,
        "bwd": attention_back,
        "kvsum": keyval_sum,
        "ffin": lambda: project(FWD, 1),
        "attF": lambda: attend(1),
        "fin0": finish_back,
        "fin1": finish_forward,
        "rcv0": get_grad,
        "rcv1": get_act,
    }
    for i in range(4):
        tasks[f"woe{i}"] = lambda i=i: make_woe(i)
        tasks[f"qe{i}"] = lambda i=i: make_qe(i)
    for a, name in enumerate("gsf"):
        for part in range(2):
            tasks[f"{name}x{part}"] = lambda a=a, part=part: swap(a, part)
            for k in range(4):
                tasks[f"{name}{part}{k}"] = lambda a=a, part=part, k=k: contract(a, part, k)
    for w, first in enumerate((back_part, fwd_part)):
        for q in range(2):
            tasks[f"sp{w}{q}"] = lambda w=w, q=q, first=first: spread(w, q, first)
            tasks[f"rx{w}{q}"] = lambda w=w, q=q: reduce_x(w, q)
            tasks[f"rz{w}{q}"] = lambda w=w, q=q: reduce_z(w, q)
    formed = set()
    for item in ORDER:
        if isinstance(item, str):
            tasks[item]()
        elif item[0] == "W":
            take(*item[1:])
        else:
            if item[1] not in formed:
                formed.add(item[1])
                form_own(item[1])
            hand(*item[1:])
    for copy in pending:
        copy.wait_send()
    for copy in stores:
        copy.wait()


def hand_over(*refs):
    for i in range(4):
        refs[4 + i][...] = refs[i][...]


def on_device(
    fwd_in, saved_in, grad_in, norm_gain, query_weight, keyval_weight, out_weight, encoder, decoder, seq_pos, rope_ids
):
    frequency = np.repeat(ROPE_BASE ** (-2.0 * np.arange(HD // 2) / HD), 2)[None].astype(np.float32)
    operands = [
        fwd_in[0],
        saved_in[0],
        grad_in[0],
        norm_gain,
        jnp.asarray(frequency),
        rope_ids[None],
        seq_pos[None],
        query_weight[0],
        keyval_weight[0].T,
        out_weight[0],
        encoder.transpose(0, 2, 1).reshape(ENC, 128),
        decoder.reshape(ENC, 128),
    ]
    hbm = pl.BlockSpec(memory_space=pl.ANY)
    vmem = pl.BlockSpec(memory_space=pltpu.VMEM)
    dma = pltpu.SemaphoreType.DMA
    shapes = [jax.ShapeDtypeStruct((8, D), BF16)] * 4
    outs = pl.pallas_call(
        kernel,
        out_shape=shapes,
        in_specs=[hbm] * len(operands),
        out_specs=[hbm] * 4,
        scratch_shapes=[pltpu.VMEM(x.shape, x.dtype) for x in operands]
        + [
            pltpu.VMEM((D // 2, 256), BF16),
            pltpu.VMEM((128, HALF), BF16),
            pltpu.VMEM((256, HALF), BF16),
        ]
        + [pltpu.VMEM((8, D), BF16)] * 4
        + [
            pltpu.VMEM((3, 2, 8, 16, HALF), BF16),
            pltpu.VMEM((T, HD), F32),
            pltpu.VMEM((T, HD), F32),
            pltpu.VMEM((T, HD), F32),
            pltpu.VMEM((T, HD), F32),
            pltpu.VMEM((T, HD), F32),
            pltpu.VMEM((8, T), F32),
            pltpu.VMEM((D, 128), BF16),
            pltpu.VMEM((ENC, 512), BF16),
            pltpu.VMEM((ENC, 512), BF16),
            pltpu.VMEM((256, ENC), BF16),
            pltpu.VMEM((ENC, 256), BF16),
            pltpu.VMEM((ENC, 64), BF16),
            pltpu.VMEM((3, 2, 8, HALF), F32),
            pltpu.VMEM((3, 2, 8, HALF), F32),
            pltpu.VMEM((8, 128), F32),
            pltpu.VMEM((3, T, 256), F32),
            pltpu.VMEM((3, T, 128), F32),
            pltpu.VMEM((3, T, 256), F32),
            pltpu.VMEM((3, T, 256), F32),
            pltpu.VMEM((3, T, 128), F32),
            pltpu.VMEM((2, 4, 64, T), BF16),
            pltpu.VMEM((2, T, 256), BF16),
            pltpu.VMEM((2, HD, T), BF16),
            pltpu.VMEM((T, 256), BF16),
            pltpu.VMEM((256, T), BF16),
            pltpu.VMEM((2, T, T), F32),
            pltpu.VMEM((T, 256), BF16),
            pltpu.VMEM((T, 256), BF16),
            pltpu.VMEM((T, 128), BF16),
            pltpu.VMEM((4, 64, T), BF16),
            pltpu.VMEM((3, 64, T), BF16),
            pltpu.VMEM((2, 2, 2, 2, 8, 16, ENC // 4), BF16),
            pltpu.VMEM((2, 2, 2, 8, 16, ENC // 4), BF16),
            pltpu.VMEM((2, 2, 8, 16, ENC // 4), BF16),
            pltpu.VMEM((2, 2, 7, 16, ENC // 4), BF16),
            pltpu.VMEM((2, 16, ENC // 2), BF16),
            pltpu.VMEM((2, 16, ENC // 2), BF16),
            pltpu.VMEM((8, D), F32),
            dma((len(operands) + 1,)),
            dma((4,)),
            dma((3,)),
            dma((3,)),
            dma((3,)),
            dma((3,)),
            dma((3, len(KEYS))),
            dma((3, len(KEYS))),
            dma((3, 2, 2)),
            dma((3, 2, 2)),
            dma((2, 3)),
            dma((2, 3)),
            dma((3,)),
            dma((3,)),
            dma((2, 2, 9)),
            dma((2, 2, 9)),
            dma((2,)),
            dma((2,)),
        ],
        compiler_params=pltpu.CompilerParams(collective_id=0, has_side_effects=True, vmem_limit_bytes=60 << 20),
        name="relay_tick",
    )(*operands)
    outs = pl.pallas_call(
        hand_over,
        out_shape=shapes,
        in_specs=[vmem] * 4,
        out_specs=[vmem] * 4,
        name="hand_over",
    )(*outs)
    return tuple(o[None] for o in outs)


def solution(mesh):
    rows = P("section", "tensor", None)
    columns = P("section", None, "tensor")
    return jax.shard_map(
        on_device,
        mesh=mesh,
        in_specs=(rows, rows, rows, P("section", None), columns, columns, rows, P(), P(), P(), P()),
        out_specs=(rows, rows, rows, rows),
        check_vma=False,
    )
```

time: 135 us -> 101 us (0.75)
  Pallas kernels: 118 us -> 100 us
  local copies, waits for them, and re-layouts: 14.9 us -> 0 us
  other arithmetic: 1.56 us -> 0 us
    pallas_call x1 -> x2, Pallas kernels: 118 us -> 100 us  [the longest x1 98.1 us: on_device(): pl.pallas_call(kernel, out_shape=shapes, in_specs=[hbm] * len(operands),...]
    unnamed x14 -> x0, local copies, waits for them, and re-layouts: 10.7 us -> none
    another operation x3 -> x0, local copies, waits for them, and re-layouts: 1.54 us -> none  [the longest x1 0.76 us: on_device(): seq[:, None]]
where the time goes in v2:
time: 101 us
  Pallas kernels  100 us (99%)
    pallas_call x1, Pallas kernels, on_device(): pl.pallas_call(kernel, out_shape=shapes, in_specs=[hbm] * len(operands),...  98.1 us

profile of v2, /device:TPU:2, one launch (start us, length us, event | category | flops | bytes accessed | tf_op | source)
XLA Modules:
  0.0 100.7 jit_solution(2817115087176073528)
XLA Ops:
  0.6 98.1 %relay_tick.1 = (bf16[8,8192]{1,0:T(8,128)(2,1)}, bf16[8,8192]{1,0:T(8,128)(2,1)}, bf16[8,8192]{1,0:T(8,128)(2,1)}, bf16[8,8192]{1,0:T(8,128)(2,1)}) custom-call(bf16[8,8192]{1,0:T(8,128)(2,1)} %bitcast.23, bf16[8,8192]{1,0:T(8,128)(2,1)} %bitcast.24, bf16[8,8192]{1,0:T(8,128)(2,1)} %bitcast.25, f32[1,8192]{1,0:T(1,128)} %gain_hbm.1, ...), custom_call_target="tpu_custom_call" | custom-call | tf_op jit(solution)/shard_map/relay_tick/pallas_call | solution.py:534
  98.8 1.9 %hand_over.1 = (bf16[8,8192]{1,0:T(8,128)(2,1)}, bf16[8,8192]{1,0:T(8,128)(2,1)}, bf16[8,8192]{1,0:T(8,128)(2,1)}, bf16[8,8192]{1,0:T(8,128)(2,1)}) custom-call(bf16[8,8192]{1,0:T(8,128)(2,1)} %get-tuple-element.12.refs_0_, bf16[8,8192]{1,0:T(8,128)(2,1)} %get-tuple-element.13.refs_1_, bf16[8,8192]{1,0:T(8,128)(2,1)} %get-tuple-element.14.refs_2_, ...), custom_call_target="tpu_custom_call" | custom-call | tf_op jit(solution)/shard_map/hand_over/pallas_call | solution.py:608

commit v3 on v2

v3 whole, which is shorter than its diff:
```python
import math

import jax
import jax.numpy as jnp
import numpy as np
from jax import lax
from jax.experimental import pallas as pl
from jax.experimental.pallas import tpu as pltpu
from jax.sharding import PartitionSpec as P

MESH = pl.DeviceIdType.MESH
HD = 128
D = 8192
HALF = D // 2
ENC = 2048
T = 256
EPSILON = 1e-05
ROPE_BASE = 10000.0
NEG_FILL = -1e30
SCALE = 1.0 / math.sqrt(HD)
F32 = jnp.float32
BF16 = jnp.bfloat16
SAVED, GRAD, FWD = 0, 1, 2
Z_FIRST = ((0, 1),)

KEYS = [(0, 1), (0, -1), (0, 2), (0, -2), (0, 3), (0, -3), (0, 4, 0), (0, 4, 1)]
KEYS += [(1, 0), (1, 1), (1, -1), (1, 2), (1, -2), (1, 3), (1, -3), (1, 4, 0), (1, 4, 1)]
COLUMNS = [[k for k in KEYS if k[0] == 0], [k for k in KEYS if k[0] == 1]]
ORDER = [
    ("S", 0, "M", (0, 0)), ("S", 0, "P", (0, 0)), ("S", 0, "X", (0, 0)), "tables", ("S", 1, "M", (0, 0)),
    ("S", 1, "P", (0, 0)), "enc", ("S", 1, "X", (0, 0)), "woe0", "woe1", ("W", 0, (0, 1)), ("S", 0, "M", (0, 1)),
    ("W", 0, (0, -1)), ("S", 0, "P", (0, -1)), "woe2", ("S", 0, "X", (0, 1)), "woe3", ("W", 1, (0, 1)),
    ("S", 1, "M", (0, 1)), ("W", 1, (0, -1)), ("S", 1, "P", (0, -1)), "qe0", "qe1", ("S", 0, "X", (0, -1)), "qe2",
    ("W", 0, (0, 2)), ("S", 0, "M", (0, 2)), ("W", 0, (0, -2)), ("S", 0, "P", (0, -2)), ("S", 0, "X", (0, 2)),
    "qe3", ("S", 2, "M", (0, 0)), ("S", 2, "P", (0, 0)), "maps", ("S", 0, "X", (0, -2)), "own", ("W", 1, (0, 2)),
    ("S", 1, "M", (0, 2)), ("W", 1, (0, -2)), ("S", 1, "P", (0, -2)), ("S", 1, "X", (0, 2)), ("W", 0, (0, 3)),
    ("S", 0, "M", (0, 3)), ("W", 0, (0, -3)), ("S", 0, "P", (0, -3)), ("W", 0, (1, 2)), ("S", 0, "M", (1, 2)),
    ("S", 1, "X", (0, -2)), ("W", 2, (0, -1)), ("S", 2, "P", (0, -1)), ("W", 2, (0, 1)), ("S", 2, "M", (0, 1)),
    ("W", 0, (1, -2)), ("S", 0, "P", (1, -2)), ("S", 1, "X", (0, 1)), ("W", 0, (0, 4, 0)), ("W", 0, (0, 4, 1)),
    "s00", "s01", "s02", ("W", 1, (0, 3)), ("S", 1, "M", (0, 3)), ("W", 1, (0, -3)), ("S", 1, "P", (0, -3)), "s03",
    "sk0", "sx0", ("W", 1, (1, 2)), ("S", 1, "M", (1, 2)), ("W", 1, (1, -2)), ("S", 1, "P", (1, -2)),
    ("W", 2, (0, -2)), ("S", 2, "X", (0, -2)), ("W", 0, (1, 3)), ("S", 0, "M", (1, 3)), ("S", 2, "P", (0, -2)),
    ("W", 2, (0, 2)), ("S", 2, "X", (0, 2)), ("S", 2, "M", (0, 2)), ("W", 1, (0, 4, 0)), ("W", 1, (0, 4, 1)),
    "g00", "g01", "g02", ("W", 0, (1, -3)), ("S", 0, "P", (1, -3)), "g03", "gx0", ("W", 1, (1, 3)),
    ("S", 1, "M", (1, 3)), ("W", 1, (1, -3)), ("S", 1, "P", (1, -3)), ("S", 1, "X", (0, -1)), ("W", 2, (1, -2)),
    ("S", 2, "P", (1, -2)), ("S", 2, "X", (0, 0)), ("W", 2, (1, 2)), ("S", 2, "M", (1, 2)), ("W", 2, (0, -3)),
    ("S", 2, "P", (0, -3)), ("W", 2, (0, 3)), ("S", 2, "M", (0, 3)), ("W", 0, (1, 0)), ("W", 0, (1, 1)),
    ("W", 0, (1, -1)), ("W", 0, (1, 4, 0)), ("W", 0, (1, 4, 1)), "s10", "s11", "s12", ("S", 2, "X", (0, 1)),
    ("W", 1, (1, 0)), ("W", 1, (1, 1)), ("W", 1, (1, -1)), ("W", 1, (1, 4, 0)), ("W", 1, (1, 4, 1)), "g10", "g11",
    "g12", "g13", "gx1", "s13", "sk1", ("W", 2, (1, 3)), ("S", 2, "M", (1, 3)), ("W", 2, (1, -3)),
    ("S", 2, "P", (1, -3)), "sx1", ("S", 2, "X", (0, -1)), ("W", 2, (0, 4, 0)), ("W", 2, (0, 4, 1)), "f00", "f01",
    "f02", "f03", "fk0", "fx0", "gfin", "sfin", "attS", "bwd", ("W", 2, (1, 0)), ("W", 2, (1, 1)),
    ("W", 2, (1, -1)), ("W", 2, (1, 4, 0)), ("W", 2, (1, 4, 1)), "f10", "f11", "f12", "f13", "fk1", "fx1", "kvsum",
    "sp01", "sp00", "ffin", "rz01", "attF", "rx00", "sp11", "sp10", "rx11", "rx10", "rz00", "rx01", "rz11", "rz10",
    "fin0", "rcv0", "fin1", "rcv1",
]


def mm(a, b):
    return jnp.dot(a, b, preferred_element_type=F32)


def mm_nt(a, b):
    return lax.dot_general(a, b, (((1,), (1,)), ((), ())), preferred_element_type=F32)


def rotate(x, cosine, sine):
    lane = lax.broadcasted_iota(jnp.int32, x.shape, 1)
    swapped = jnp.where(lane % 2 == 0, pltpu.roll(x, x.shape[1] - 1, 1), pltpu.roll(x, 1, 1))
    return x * cosine + swapped * sine


def kernel(
    fwd_hbm, saved_hbm, grad_hbm, gain_hbm, freq_hbm, rope_hbm, seq_hbm, wq_hbm, wkv_hbm, wo_hbm, enc_hbm, dec_hbm,
    out_hbm, act_hbm, ig_hbm, gs_hbm,
    fwd_ref, saved_ref, grad_ref, gain_ref, freq_ref, rope_ref, seq_ref, wq, wkv, wo, enc_raw, dec_raw, wqs, wos,
    out_ref, act_ref, ig_ref, gs_ref,
    G, cos_ref, sin_ref, kvcos_ref, kvsin_ref, seqc_ref, seqr_ref, enc_bd, enc_t, dec_bd, woe, qe, kve, de, dge, enc_fwd, enc_saved, enc_grad, pull_ref,
    nrm, chipf, factor_ref, acc, acckv, other, got, kvp, kvt, qrot, qtr, gab, gatr, prob, att, qg, kvg, kgs, kgr,
    rsb, r1, r2, r3, rz, rz1, rz3, rz2, pk_s, pk_r,
    wsem, osem, ws_s, ws_r, st_s, st_r, g_s, g_r, sb_s, sb_r, kv_s, kv_r, kg_s, kg_r, rs_s, rs_r, sc_s, sc_r,
):
    s = lax.axis_index("section")
    t = lax.axis_index("tensor")
    z, h, c = t // 4, (t // 2) % 2, t % 2

    def tid(zz, hh, cc):
        return (s, zz * 4 + hh * 2 + cc)

    def zmod(d):
        return lax.rem(z + d + 8, 8)

    sib = tid(z, h, 1 - c)
    link = {"M": tid(zmod(-1), h, c), "P": tid(zmod(1), h, c), "X": tid(z, 1 - h, c)}
    group = [sib, link["X"], tid(z, 1 - h, 1 - c)]
    nxt, prv = (lax.rem(s + 1, 8), t), (lax.rem(s + 7, 8), t)
    along = [tid(zmod(k), h, c) for k in range(1, 8)]

    arrays = {
        "saved": (saved_hbm, saved_ref), "gain": (gain_hbm, gain_ref), "grad": (grad_hbm, grad_ref), "fwd": (fwd_hbm, fwd_ref),
        "rope": (rope_hbm, rope_ref), "seq": (seq_hbm, seq_ref), "freq": (freq_hbm, freq_ref),
        "enc": (enc_hbm, enc_raw), "dec": (dec_hbm, dec_raw), "wo": (wo_hbm, wo), "wq": (wq_hbm, wq), "wkv": (wkv_hbm, wkv.at[c]),
    }
    loads = {}
    for i, (name, (src, dst)) in enumerate(arrays.items()):
        loads[name] = pltpu.make_async_copy(src, dst, wsem.at[i])
        loads[name].start()

    barrier = pltpu.get_barrier_semaphore()
    for peer in along + group + [nxt, prv]:
        pl.semaphore_signal(barrier, inc=1, device_id=peer, device_id_type=MESH)

    def put_own(a, values):
        nrm[a, 0] = values[:, :HALF]
        nrm[a, 1] = values[:, HALF:]

    def normed(ref, slot):
        x = ref[...].astype(F32)
        factor = lax.rsqrt(jnp.mean(x * x, axis=-1, keepdims=True) + EPSILON)
        if slot is not None:
            factor_ref[...] = jnp.broadcast_to(factor, factor_ref.shape)
        return x * factor * gain_ref[...]

    pending, stores = [], []

    def store(i, src, dst):
        stores.append(pltpu.make_async_copy(src, dst, osem.at[i]))
        stores[-1].start()

    def send(src, dst, ssem, rsem, peer):
        copy = pltpu.make_async_remote_copy(
            src_ref=src, dst_ref=dst, send_sem=ssem, recv_sem=rsem, device_id=peer, device_id_type=MESH
        )
        copy.start()
        pending.append(copy)

    def arrived(dst, ssem, rsem, peer):
        pltpu.make_async_remote_copy(
            src_ref=dst, dst_ref=dst, send_sem=ssem, recv_sem=rsem, device_id=peer, device_id_type=MESH
        ).wait_recv()

    def stage(a):
        send(nrm.at[a, 1 - c], chipf.at[a, c], st_s.at[a], st_r.at[a], sib)

    loads["saved"].wait()
    loads["gain"].wait()
    put_own(SAVED, normed(saved_ref, 0))
    pl.semaphore_wait(barrier, len(along) + len(group) + 2)
    stage(SAVED)
    loads["grad"].wait()
    put_own(GRAD, grad_ref[...].astype(F32))
    stage(GRAD)
    loads["fwd"].wait()
    put_own(FWD, normed(fwd_ref, None))
    stage(FWD)

    away = pl.ds(pl.multiple_of((1 - c) * HALF, HALF), HALF)
    shared = [(wq_hbm.at[away, :], wqs), (wkv_hbm, wkv.at[c]), (wo_hbm.at[:, away], wos)]
    for i, (src, dst) in enumerate(shared):
        send(src, dst, ws_s.at[i], ws_r.at[i], sib)

    ready = set()

    def need(*names):
        for name in names:
            if name in ready:
                continue
            ready.add(name)
            if isinstance(name, int):
                dst = wkv.at[1 - c] if name == 1 else shared[name][1]
                arrived(dst, ws_s.at[name], ws_r.at[name], sib)
            else:
                loads[name].wait()

    def make_tables():
        need("rope", "seq", "freq")

        def down(row):
            tall = jnp.broadcast_to(row.astype(F32), (128, T)).T
            return jnp.concatenate([tall[zz * 32 + hh * 16 :][:16] for hh in range(2) for zz in range(8)], axis=0)

        positions = down(seq_ref[...])
        seqc_ref[...] = positions
        seqr_ref[...] = positions.T[:8]
        angle = down(rope_ref[...]) * freq_ref[...]
        cosine, sine = jnp.cos(angle), jnp.sin(angle)
        sine = jnp.where(lax.broadcasted_iota(jnp.int32, sine.shape, 1) % 2 == 0, -sine, sine)
        cos_ref[...] = cosine
        sin_ref[...] = sine
        is_key = jnp.where(h == 0, 1.0, 0.0)
        kvcos_ref[...] = is_key * cosine + (1.0 - is_key)
        kvsin_ref[...] = is_key * sine

    def where(key):
        return (h if key[0] == 0 else 1 - h), zmod(key[1])

    def piece(a, key):
        ref = G.at[(a, *where(key))]
        if len(key) == 3:
            ref = ref.at[:, pl.ds(key[2] * (HALF // 2), HALF // 2)]
        return ref

    def form_own(a):
        arrived(chipf.at[a, 1 - c], st_s.at[a], st_r.at[a], sib)
        chipf[a, c] = nrm[a, c]
        G[a, h, z] = chipf[a].reshape(16, HALF).astype(BF16)

    def take(a, key):
        i = KEYS.index(key)
        arrived(piece(a, key), g_s.at[a, i], g_r.at[a, i], link["M"])

    def hand(a, way, key):
        column, far = (key[0], key[1] + (1 if way == "M" else -1)) if way != "X" else (1 - key[0], key[1])
        there = (column, 4, 0 if way == "M" else 1) if abs(far) == 4 else (column, far)
        i = KEYS.index(there)
        part = piece(a, key + there[2:])
        send(part, part, g_s.at[a, i], g_r.at[a, i], link[way])

    def make_enc():
        need("enc", "dec")

        def fill(i, _):
            rows = pl.ds(i * 128, 128)
            group_row = lax.broadcasted_iota(jnp.int32, (128, 128), 0) // 32
            e, d = enc_raw[rows, :], dec_raw[rows, :]
            wide = jnp.concatenate([jnp.where(group_row == q, e, 0.0) for q in range(4)], axis=1)
            enc_t[rows, :] = wide.astype(BF16)
            enc_bd[pl.ds(i * 512, 512), :] = wide.T.astype(BF16)
            wide = jnp.concatenate([jnp.where(group_row == q, d, 0.0) for q in range(4)], axis=1)
            dec_bd[rows, :] = wide.astype(BF16)
            return 0

        lax.fori_loop(0, 16, fill, 0)

    def make_woe(part):
        need("wo")

        def fill(i, _):
            cols = pl.ds(pl.multiple_of(i * 512, 512), 512)
            outs = pl.ds(pl.multiple_of(i * 128, 128), 128)
            woe[:, outs] = mm(wo[:, cols], enc_bd[pl.ds(i * 512, 512), :]).astype(BF16)
            return 0

        lax.fori_loop(part * 4, part * 4 + 4, fill, 0)

    def make_qe(part):
        need("wq", "wkv", 1)

        def fill(i, _):
            rows, outs = pl.ds(i * 512, 512), pl.ds(i * 128, 128)
            e = enc_t[outs, :]
            qe[outs, :] = mm(e, wq[rows, :]).astype(BF16)
            kve[outs, :] = mm_nt(e, wkv[:, :, pl.ds(pl.multiple_of(i * 512, 512), 512)].reshape(128, 512)).astype(BF16)
            return 0

        lax.fori_loop(part * 4, part * 4 + 4, fill, 0)

    def rows_of(part):
        return pl.ds(pl.multiple_of((h if part == 0 else 1 - h) * 128, 128), 128)

    def contract(a, part, k):
        need(*(("wo", 2) if a == GRAD else ("wq", "wkv", 0, 1)))
        rows, cols = rows_of(part), slice(k * 1024, k * 1024 + 1024)
        here = pl.ds(pl.multiple_of(c * HALF + k * 1024, 1024), 1024)
        x = G[a, h if part == 0 else 1 - h, :, :, cols].reshape(128, 1024)
        if a == GRAD:
            products = [(acc, mm_nt(x, wo[:, here])), (other, mm_nt(x, wos[:, cols]))]
        else:
            products = [(acc, mm(x, wq[here, :])), (other, mm(x, wqs[cols, :])), (acckv, mm_nt(x, wkv[:, :, here].reshape(128, 1024)))]
        for ref, product in products:
            if k == 0:
                ref[a, rows, :] = product
            else:
                ref[a, rows, :] += product

    def swap(a, part):
        rows = rows_of(part)
        send(other.at[a, rows], got.at[a, rows], sb_s.at[a, part], sb_r.at[a, part], sib)

    def swapped(a):
        for part in range(2):
            rows = rows_of(part)
            arrived(got.at[a, rows], sb_s.at[a, part], sb_r.at[a, part], sib)

    def keyvals(a, w, part):
        rows, col = rows_of(part), h if part == 0 else 1 - h
        turned = rotate(acckv[a, rows, :], kvcos_ref[rows, :], kvsin_ref[rows, :])
        mine = kvp.at[w, h, c, col]
        mine[...] = turned.T.astype(BF16)
        for i, peer in enumerate(group):
            send(mine, mine, kv_s.at[w, part, i], kv_r.at[w, part, i], peer)

    def keyvals_in(w):
        for part in range(2):
            col = h if part == 0 else 1 - h
            for i, (hh, cc) in enumerate([(h, 1 - c), (1 - h, c), (1 - h, 1 - c)]):
                arrived(kvp.at[w, hh, cc, col], kv_s.at[w, part, i], kv_r.at[w, part, i], group[i])
        for hh in range(2):
            for col in range(2):
                total = kvp[w, hh, 0, col].astype(F32) + kvp[w, hh, 1, col].astype(F32)
                kvt[w, hh, :, col * 128 : col * 128 + 128] = total.astype(BF16)

    def project(a, w):
        swapped(a)
        for i in range(2):
            cols = slice(i * HD, (i + 1) * HD)
            q = rotate(acc[a, :, cols] + got[a, :, cols], cos_ref[...], sin_ref[...])
            qrot[w, :, cols] = q.astype(BF16)
            if w == 0:
                qtr[i] = q.T.astype(BF16)

    def attend(w):
        keyvals_in(w)
        kt, vt = kvt[w, 0], kvt[w, 1]
        visible = seqr_ref[:1, :] <= seqc_ref[:, :1]
        for i in range(2):
            cols = slice(i * HD, (i + 1) * HD)
            scores = jnp.where(visible, mm(qrot[w, :, cols], kt) * SCALE, NEG_FILL)
            raised = jnp.exp(scores - jnp.max(scores, axis=-1, keepdims=True))
            p = raised / jnp.sum(raised, axis=-1, keepdims=True)
            if w == 0:
                prob[i] = p
            else:
                att[:, cols] = mm_nt(p.astype(BF16), vt).astype(BF16)

    def grad_attended():
        swapped(GRAD)
        total = acc[GRAD] + got[GRAD]
        gab[...] = total.astype(BF16)
        gatr[...] = total.T.astype(BF16)

    def attention_back():
        kt, vt = kvt[0, 0], kvt[0, 1]
        key_sum = jnp.zeros((HD, T), F32)
        value_sum = jnp.zeros((HD, T), F32)
        for i in range(2):
            cols = slice(i * HD, (i + 1) * HD)
            p = prob[i]
            dp = mm(gab[:, cols], vt)
            sg = (p * (dp - jnp.sum(p * dp, axis=-1, keepdims=True)) * SCALE).astype(BF16)
            qg[:, cols] = rotate(mm_nt(sg, kt), cos_ref[...], -sin_ref[...]).astype(BF16)
            key_sum += mm(qtr[i], sg)
            value_sum += mm(gatr[cols, :], p.astype(BF16))
        kgs[0] = key_sum.astype(BF16)
        kgs[1] = value_sum.astype(BF16)
        send(kgs.at[1 - h], kgr, kg_s, kg_r, link["X"])

    def keyval_sum():
        arrived(kgr, kg_s, kg_r, link["X"])
        total = kgs[h].astype(F32) + kgr[...].astype(F32)
        kvg[...] = rotate(total.T, kvcos_ref[...], -kvsin_ref[...]).astype(BF16)

    def spread(w, q, first):
        def chunk(k, _):
            at = pl.multiple_of(q * 512 + k * 256, 256)
            lows, highs = first(at), first(at + ENC // 2)
            cols = pl.ds(pl.multiple_of(k * 256, 256), 256)
            for b in range(32):
                hh, zz, cc = b // 16, (b // 2) % 8, b % 2
                rows = slice(b * 8, b * 8 + 8)
                both = jnp.concatenate([lows[rows], highs[rows]], axis=0).astype(BF16)
                if (w, q) in Z_FIRST:
                    rz[w, q, cc, zz, hh, :, cols] = both
                else:
                    rsb[w, q, cc, hh, zz, :, cols] = both
            return 0

        lax.fori_loop(0, 2, chunk, 0)
        src, dst = (rz, rz1) if (w, q) in Z_FIRST else (rsb, r1)
        send(src.at[w, q, 1 - c], dst.at[w, q], rs_s.at[w, q, 0], rs_r.at[w, q, 0], sib)

    def fwd_part(at):
        return mm(att[...], woe[:, pl.ds(at, 256)])

    def back_part(at):
        return mm_nt(qg[...], qe[pl.ds(at, 256), :]) + mm_nt(kvg[...], kve[pl.ds(at, 256), :])

    def from_core(w, q):
        arrived((rz1 if (w, q) in Z_FIRST else r1).at[w, q], rs_s.at[w, q, 0], rs_r.at[w, q, 0], sib)

    def along_z(w, q, slots, total):
        for k in range(1, 8):
            arrived(slots.at[w, q, k - 1], rs_s.at[w, q, 1 + k], rs_r.at[w, q, 1 + k], along[k - 1])
            total += slots[w, q, k - 1].astype(F32)
        return total

    def reduce_x(w, q):
        sems = rs_s.at[w, q, 1], rs_r.at[w, q, 1]
        if (w, q) in Z_FIRST:
            rz[w, q, c, z] = along_z(w, q, rz3, rz[w, q, c, z].astype(F32)).astype(BF16)
            send(rz.at[w, q, c, z, 1 - h], rz2.at[w, q], *sems, link["X"])
        else:
            from_core(w, q)
            rsb[w, q, c, 1 - h] = (rsb[w, q, c, 1 - h].astype(F32) + r1[w, q, 1 - h].astype(F32)).astype(BF16)
            send(rsb.at[w, q, c, 1 - h], r2.at[w, q], *sems, link["X"])

    def reduce_z(w, q):
        if (w, q) in Z_FIRST:
            from_core(w, q)
            rz[w, q, c] = (rz[w, q, c].astype(F32) + rz1[w, q].astype(F32)).astype(BF16)
        else:
            arrived(r2.at[w, q], rs_s.at[w, q, 1], rs_r.at[w, q, 1], link["X"])
            total = rsb[w, q, c, h].astype(F32) + r1[w, q, h].astype(F32) + r2[w, q].astype(F32)
            rsb[w, q, c, h] = total.astype(BF16)
        for k in (4, 3, 5, 2, 6, 1, 7):
            sems = rs_s.at[w, q, 1 + k], rs_r.at[w, q, 1 + k]
            if (w, q) in Z_FIRST:
                send(rz.at[w, q, c, zmod(k)], rz3.at[w, q, k - 1], *sems, along[k - 1])
            else:
                send(rsb.at[w, q, c, h, zmod(k)], r3.at[w, q, k - 1], *sems, along[k - 1])

    def reduced(w):
        totals = []
        for q in range(2):
            if (w, q) in Z_FIRST:
                arrived(rz2.at[w, q], rs_s.at[w, q, 1], rs_r.at[w, q, 1], link["X"])
                totals.append(rz[w, q, c, z, h].astype(F32) + rz2[w, q].astype(F32))
            else:
                totals.append(along_z(w, q, r3, rsb[w, q, c, h, z].astype(F32)))
        return jnp.concatenate(totals, axis=1)

    def part_of(i):
        return slice((i // 8) * 8, (i // 8) * 8 + 8), slice((i % 8) * 128, (i % 8) * 128 + 128)

    def wide(i):
        return slice(i * 512, i * 512 + 512)

    def each_group(make):
        return [jnp.concatenate([make(i), make(i + 8)], axis=0) for i in range(8)]

    def decode_piece(encoded, i):
        return mm(encoded[part_of(i)].astype(BF16), dec_bd[i * 128 : i * 128 + 128, :])

    def make_maps():
        def fill(i, _):
            rows, cols = pl.ds(i * 128, 128), pl.ds(pl.multiple_of(i * 512, 512), 512)
            d, e = dec_bd[rows, :], enc_bd[pl.ds(i * 512, 512), :]
            de[rows, :] = mm(d, e).astype(BF16)
            dge[rows, :] = mm((d.astype(F32) * gain_ref[:, cols]).astype(BF16), e).astype(BF16)
            return 0

        lax.fori_loop(0, 16, fill, 0)

    def make_encoded():
        def encode(ref):
            return each_group(lambda i: mm(ref[:, wide(i)], enc_bd[i * 512 : i * 512 + 512, :]))

        def pull(i):
            x = saved_ref[:, wide(i)].astype(F32) * gain_ref[:, wide(i)]
            return mm_nt(x.astype(BF16), dec_bd[i * 128 : i * 128 + 128, :])

        for i, parts in enumerate(zip(encode(fwd_ref), encode(saved_ref), encode(grad_ref), each_group(pull))):
            for ref, value in zip((enc_fwd, enc_saved, enc_grad, pull_ref), parts):
                ref[:, i * 128 : i * 128 + 128] = value

    def pack(w, values, peer):
        pk_s[w] = values.astype(BF16)
        send(pk_s.at[w], pk_r.at[w], sc_s.at[w], sc_r.at[w], peer)

    def mapped(total, table):
        parts = each_group(lambda i: mm(total[part_of(i)].astype(BF16), table[i * 128 : i * 128 + 128, :]))
        return jnp.concatenate(parts, axis=1)

    def received(w, out, peer, keep):
        arrived(pk_r.at[w], sc_s.at[w], sc_r.at[w], peer)
        got = pk_r[w].astype(F32)
        got = got * jnp.where(keep, 1.0, 0.0)
        for i in range(16):
            out[:, wide(i)] = decode_piece(got, i).astype(BF16)

    def finish_forward():
        total = reduced(1)
        pack(1, enc_fwd[...] + mapped(total, de), nxt)
        for i in range(16):
            out_ref[:, wide(i)] = (fwd_ref[:, wide(i)].astype(F32) + decode_piece(total, i)).astype(BF16)
        store(0, out_ref, out_hbm)

    def finish_back():
        total = reduced(0)
        dots = jnp.sum(total * pull_ref[...], axis=-1, keepdims=True)
        factor = factor_ref[:, :1]
        pull = factor * factor * ((dots[:8] + dots[8:]) * (1.0 / D))
        both = jnp.concatenate([factor, factor], axis=0), jnp.concatenate([pull, pull], axis=0)
        pack(0, enc_grad[...] + both[0] * (mapped(total, dge) - both[1] * enc_saved[...]), prv)
        for i in range(16):
            x = saved_ref[:, wide(i)].astype(F32)
            scaled = decode_piece(total, i) * gain_ref[:, wide(i)]
            value = grad_ref[:, wide(i)].astype(F32) + factor * (scaled - x * pull)
            ig_ref[:, wide(i)] = value.astype(BF16)
        store(2, ig_ref, ig_hbm)

    def get_grad():
        received(0, gs_ref, nxt, s < 7)
        store(3, gs_ref, gs_hbm)

    def get_act():
        received(1, act_ref, prv, s > 0)
        store(1, act_ref, act_hbm)

    tasks = {
        "tables": make_tables,
        "enc": make_enc,
        "maps": make_maps,
        "own": make_encoded,
        "sfin": lambda: project(SAVED, 0),
        "attS": lambda: attend(0),
        "gfin": grad_attended,
        "bwd": attention_back,
        "kvsum": keyval_sum,
        "ffin": lambda: project(FWD, 1),
        "attF": lambda: attend(1),
        "fin0": finish_back,
        "fin1": finish_forward,
        "rcv0": get_grad,
        "rcv1": get_act,
    }
    for i in range(4):
        tasks[f"woe{i}"] = lambda i=i: make_woe(i)
        tasks[f"qe{i}"] = lambda i=i: make_qe(i)
    for a, name in ((SAVED, "s"), (GRAD, "g"), (FWD, "f")):
        for part in range(2):
            tasks[f"{name}x{part}"] = lambda a=a, part=part: swap(a, part)
            for k in range(4):
                tasks[f"{name}{part}{k}"] = lambda a=a, part=part, k=k: contract(a, part, k)
    for name, a, w in (("s", SAVED, 0), ("f", FWD, 1)):
        for part in range(2):
            tasks[f"{name}k{part}"] = lambda a=a, w=w, part=part: keyvals(a, w, part)
    for w, first in enumerate((back_part, fwd_part)):
        for q in range(2):
            tasks[f"sp{w}{q}"] = lambda w=w, q=q, first=first: spread(w, q, first)
            tasks[f"rx{w}{q}"] = lambda w=w, q=q: reduce_x(w, q)
            tasks[f"rz{w}{q}"] = lambda w=w, q=q: reduce_z(w, q)
    formed = set()
    for item in ORDER:
        if isinstance(item, str):
            tasks[item]()
        elif item[0] == "W":
            take(*item[1:])
        else:
            if item[1] not in formed:
                formed.add(item[1])
                form_own(item[1])
            hand(*item[1:])
    for copy in pending:
        copy.wait_send()
    for copy in stores:
        copy.wait()


def hand_over(*refs):
    for i in range(4):
        refs[4 + i][...] = refs[i][...]


def on_device(
    fwd_in, saved_in, grad_in, norm_gain, query_weight, keyval_weight, out_weight, encoder, decoder, seq_pos, rope_ids
):
    frequency = np.repeat(ROPE_BASE ** (-2.0 * np.arange(HD // 2) / HD), 2)[None].astype(np.float32)
    operands = [
        fwd_in[0],
        saved_in[0],
        grad_in[0],
        norm_gain,
        jnp.asarray(frequency),
        rope_ids[None],
        seq_pos[None],
        query_weight[0],
        keyval_weight[0].T,
        out_weight[0],
        encoder.transpose(0, 2, 1).reshape(ENC, 128),
        decoder.reshape(ENC, 128),
    ]
    hbm = pl.BlockSpec(memory_space=pl.ANY)
    vmem = pl.BlockSpec(memory_space=pltpu.VMEM)
    dma = pltpu.SemaphoreType.DMA
    shapes = [jax.ShapeDtypeStruct((8, D), BF16)] * 4
    outs = pl.pallas_call(
        kernel,
        out_shape=shapes,
        in_specs=[hbm] * len(operands),
        out_specs=[hbm] * 4,
        scratch_shapes=[pltpu.VMEM((2, *x.shape) if x.shape[0] == 64 else x.shape, x.dtype) for x in operands]
        + [
            pltpu.VMEM((D // 2, 256), BF16),
            pltpu.VMEM((256, HALF), BF16),
        ]
        + [pltpu.VMEM((8, D), BF16)] * 4
        + [
            pltpu.VMEM((3, 2, 8, 16, HALF), BF16),
            pltpu.VMEM((T, HD), F32),
            pltpu.VMEM((T, HD), F32),
            pltpu.VMEM((T, HD), F32),
            pltpu.VMEM((T, HD), F32),
            pltpu.VMEM((T, HD), F32),
            pltpu.VMEM((8, T), F32),
            pltpu.VMEM((D, 128), BF16),
            pltpu.VMEM((ENC, 512), BF16),
            pltpu.VMEM((ENC, 512), BF16),
            pltpu.VMEM((256, ENC), BF16),
            pltpu.VMEM((ENC, 256), BF16),
            pltpu.VMEM((ENC, 128), BF16),
            pltpu.VMEM((ENC, 128), BF16),
            pltpu.VMEM((ENC, 128), BF16),
            pltpu.VMEM((16, ENC // 2), F32),
            pltpu.VMEM((16, ENC // 2), F32),
            pltpu.VMEM((16, ENC // 2), F32),
            pltpu.VMEM((16, ENC // 2), F32),
            pltpu.VMEM((3, 2, 8, HALF), F32),
            pltpu.VMEM((3, 2, 8, HALF), F32),
            pltpu.VMEM((8, 128), F32),
            pltpu.VMEM((3, T, 256), F32),
            pltpu.VMEM((3, T, 128), F32),
            pltpu.VMEM((3, T, 256), F32),
            pltpu.VMEM((3, T, 256), F32),
            pltpu.VMEM((2, 2, 2, 2, HD, 128), BF16),
            pltpu.VMEM((2, 2, HD, T), BF16),
            pltpu.VMEM((2, T, 256), BF16),
            pltpu.VMEM((2, HD, T), BF16),
            pltpu.VMEM((T, 256), BF16),
            pltpu.VMEM((256, T), BF16),
            pltpu.VMEM((2, T, T), F32),
            pltpu.VMEM((T, 256), BF16),
            pltpu.VMEM((T, 256), BF16),
            pltpu.VMEM((T, 128), BF16),
            pltpu.VMEM((2, HD, T), BF16),
            pltpu.VMEM((HD, T), BF16),
            pltpu.VMEM((2, 2, 2, 2, 8, 16, ENC // 4), BF16),
            pltpu.VMEM((2, 2, 2, 8, 16, ENC // 4), BF16),
            pltpu.VMEM((2, 2, 8, 16, ENC // 4), BF16),
            pltpu.VMEM((2, 2, 7, 16, ENC // 4), BF16),
            pltpu.VMEM((2, 2, 2, 8, 2, 16, ENC // 4), BF16),
            pltpu.VMEM((2, 2, 8, 2, 16, ENC // 4), BF16),
            pltpu.VMEM((2, 2, 7, 2, 16, ENC // 4), BF16),
            pltpu.VMEM((2, 2, 16, ENC // 4), BF16),
            pltpu.VMEM((2, 16, ENC // 2), BF16),
            pltpu.VMEM((2, 16, ENC // 2), BF16),
            dma((len(operands),)),
            dma((4,)),
            dma((3,)),
            dma((3,)),
            dma((3,)),
            dma((3,)),
            dma((3, len(KEYS))),
            dma((3, len(KEYS))),
            dma((3, 2)),
            dma((3, 2)),
            dma((2, 2, 3)),
            dma((2, 2, 3)),
            dma(()),
            dma(()),
            dma((2, 2, 9)),
            dma((2, 2, 9)),
            dma((2,)),
            dma((2,)),
        ],
        compiler_params=pltpu.CompilerParams(collective_id=0, has_side_effects=True, vmem_limit_bytes=60 << 20),
        name="relay_tick",
    )(*operands)
    outs = pl.pallas_call(
        hand_over,
        out_shape=shapes,
        in_specs=[vmem] * 4,
        out_specs=[vmem] * 4,
        name="hand_over",
    )(*outs)
    return tuple(o[None] for o in outs)


def solution(mesh):
    rows = P("section", "tensor", None)
    columns = P("section", None, "tensor")
    return jax.shard_map(
        on_device,
        mesh=mesh,
        in_specs=(rows, rows, rows, P("section", None), columns, columns, rows, P(), P(), P(), P()),
        out_specs=(rows, rows, rows, rows),
        check_vma=False,
    )
```

time: 101 us -> 93.1 us (0.922)
  Pallas kernels: 100 us -> 92.3 us
    pallas_call x1, Pallas kernels: 98.1 us -> 90.4 us  [on_device(): pl.pallas_call(kernel, out_shape=shapes, in_specs=[hbm] * len(operands),...]
where the time goes in v3:
time: 93.1 us; the launch traced here: 93 us
  Pallas kernels  92.3 us (99%)
    pallas_call x1, Pallas kernels, on_device(): pl.pallas_call(kernel, out_shape=shapes, in_specs=[hbm] * len(operands),...  90.4 us
    pallas_call x1, Pallas kernels, on_device(): pl.pallas_call(hand_over, out_shape=shapes, in_specs=[vmem] * 4, out_spec...  1.89 us

profile of v3, /device:TPU:2, one launch (start us, length us, event | category | flops | bytes accessed | tf_op | source)
XLA Modules:
  0.0 93.0 jit_solution(13222692921556624708)
XLA Ops:
  0.6 90.4 %relay_tick.1 = (bf16[8,8192]{1,0:T(8,128)(2,1)}, bf16[8,8192]{1,0:T(8,128)(2,1)}, bf16[8,8192]{1,0:T(8,128)(2,1)}, bf16[8,8192]{1,0:T(8,128)(2,1)}) custom-call(bf16[8,8192]{1,0:T(8,128)(2,1)} %bitcast.23, bf16[8,8192]{1,0:T(8,128)(2,1)} %bitcast.24, bf16[8,8192]{1,0:T(8,128)(2,1)} %bitcast.25, f32[1,8192]{1,0:T(1,128)} %gain_hbm.1, ...), custom_call_target="tpu_custom_call" | custom-call | tf_op jit(solution)/shard_map/relay_tick/pallas_call | solution.py:577
  91.1 1.9 %hand_over.1 = (bf16[8,8192]{1,0:T(8,128)(2,1)}, bf16[8,8192]{1,0:T(8,128)(2,1)}, bf16[8,8192]{1,0:T(8,128)(2,1)}, bf16[8,8192]{1,0:T(8,128)(2,1)}) custom-call(bf16[8,8192]{1,0:T(8,128)(2,1)} %get-tuple-element.12.refs_0_, bf16[8,8192]{1,0:T(8,128)(2,1)} %get-tuple-element.13.refs_1_, bf16[8,8192]{1,0:T(8,128)(2,1)} %get-tuple-element.14.refs_2_, ...), custom_call_target="tpu_custom_call" | custom-call | tf_op jit(solution)/shard_map/hand_over/pallas_call | solution.py:659

commit v4 on v3

--- a/solution.py
+++ b/solution.py
@@ -21,38 +21,38 @@
 F32 = jnp.float32
 BF16 = jnp.bfloat16
 SAVED, GRAD, FWD = 0, 1, 2
-Z_FIRST = ((0, 1),)
+Z_FIRST = ((1, 1),)
 
 KEYS = [(0, 1), (0, -1), (0, 2), (0, -2), (0, 3), (0, -3), (0, 4, 0), (0, 4, 1)]
 KEYS += [(1, 0), (1, 1), (1, -1), (1, 2), (1, -2), (1, 3), (1, -3), (1, 4, 0), (1, 4, 1)]
 COLUMNS = [[k for k in KEYS if k[0] == 0], [k for k in KEYS if k[0] == 1]]
 ORDER = [
     ("S", 0, "M", (0, 0)), ("S", 0, "P", (0, 0)), ("S", 0, "X", (0, 0)), "tables", ("S", 1, "M", (0, 0)),
-    ("S", 1, "P", (0, 0)), "enc", ("S", 1, "X", (0, 0)), "woe0", "woe1", ("W", 0, (0, 1)), ("S", 0, "M", (0, 1)),
-    ("W", 0, (0, -1)), ("S", 0, "P", (0, -1)), "woe2", ("S", 0, "X", (0, 1)), "woe3", ("W", 1, (0, 1)),
-    ("S", 1, "M", (0, 1)), ("W", 1, (0, -1)), ("S", 1, "P", (0, -1)), "qe0", "qe1", ("S", 0, "X", (0, -1)), "qe2",
-    ("W", 0, (0, 2)), ("S", 0, "M", (0, 2)), ("W", 0, (0, -2)), ("S", 0, "P", (0, -2)), ("S", 0, "X", (0, 2)),
-    "qe3", ("S", 2, "M", (0, 0)), ("S", 2, "P", (0, 0)), "maps", ("S", 0, "X", (0, -2)), "own", ("W", 1, (0, 2)),
-    ("S", 1, "M", (0, 2)), ("W", 1, (0, -2)), ("S", 1, "P", (0, -2)), ("S", 1, "X", (0, 2)), ("W", 0, (0, 3)),
-    ("S", 0, "M", (0, 3)), ("W", 0, (0, -3)), ("S", 0, "P", (0, -3)), ("W", 0, (1, 2)), ("S", 0, "M", (1, 2)),
-    ("S", 1, "X", (0, -2)), ("W", 2, (0, -1)), ("S", 2, "P", (0, -1)), ("W", 2, (0, 1)), ("S", 2, "M", (0, 1)),
-    ("W", 0, (1, -2)), ("S", 0, "P", (1, -2)), ("S", 1, "X", (0, 1)), ("W", 0, (0, 4, 0)), ("W", 0, (0, 4, 1)),
-    "s00", "s01", "s02", ("W", 1, (0, 3)), ("S", 1, "M", (0, 3)), ("W", 1, (0, -3)), ("S", 1, "P", (0, -3)), "s03",
-    "sk0", "sx0", ("W", 1, (1, 2)), ("S", 1, "M", (1, 2)), ("W", 1, (1, -2)), ("S", 1, "P", (1, -2)),
-    ("W", 2, (0, -2)), ("S", 2, "X", (0, -2)), ("W", 0, (1, 3)), ("S", 0, "M", (1, 3)), ("S", 2, "P", (0, -2)),
-    ("W", 2, (0, 2)), ("S", 2, "X", (0, 2)), ("S", 2, "M", (0, 2)), ("W", 1, (0, 4, 0)), ("W", 1, (0, 4, 1)),
-    "g00", "g01", "g02", ("W", 0, (1, -3)), ("S", 0, "P", (1, -3)), "g03", "gx0", ("W", 1, (1, 3)),
-    ("S", 1, "M", (1, 3)), ("W", 1, (1, -3)), ("S", 1, "P", (1, -3)), ("S", 1, "X", (0, -1)), ("W", 2, (1, -2)),
-    ("S", 2, "P", (1, -2)), ("S", 2, "X", (0, 0)), ("W", 2, (1, 2)), ("S", 2, "M", (1, 2)), ("W", 2, (0, -3)),
-    ("S", 2, "P", (0, -3)), ("W", 2, (0, 3)), ("S", 2, "M", (0, 3)), ("W", 0, (1, 0)), ("W", 0, (1, 1)),
-    ("W", 0, (1, -1)), ("W", 0, (1, 4, 0)), ("W", 0, (1, 4, 1)), "s10", "s11", "s12", ("S", 2, "X", (0, 1)),
-    ("W", 1, (1, 0)), ("W", 1, (1, 1)), ("W", 1, (1, -1)), ("W", 1, (1, 4, 0)), ("W", 1, (1, 4, 1)), "g10", "g11",
-    "g12", "g13", "gx1", "s13", "sk1", ("W", 2, (1, 3)), ("S", 2, "M", (1, 3)), ("W", 2, (1, -3)),
-    ("S", 2, "P", (1, -3)), "sx1", ("S", 2, "X", (0, -1)), ("W", 2, (0, 4, 0)), ("W", 2, (0, 4, 1)), "f00", "f01",
-    "f02", "f03", "fk0", "fx0", "gfin", "sfin", "attS", "bwd", ("W", 2, (1, 0)), ("W", 2, (1, 1)),
-    ("W", 2, (1, -1)), ("W", 2, (1, 4, 0)), ("W", 2, (1, 4, 1)), "f10", "f11", "f12", "f13", "fk1", "fx1", "kvsum",
-    "sp01", "sp00", "ffin", "rz01", "attF", "rx00", "sp11", "sp10", "rx11", "rx10", "rz00", "rx01", "rz11", "rz10",
-    "fin0", "rcv0", "fin1", "rcv1",
+    ("S", 1, "P", (0, 0)), ("S", 1, "X", (0, 0)), "enc", ("S", 2, "M", (0, 0)), ("S", 2, "P", (0, 0)),
+    ("S", 2, "X", (0, 0)), "woe0", ("W", 0, (0, 1)), ("S", 0, "M", (0, 1)), ("W", 0, (0, -1)),
+    ("S", 0, "P", (0, -1)), ("S", 0, "X", (0, 1)), "woe1", "woe2", ("S", 0, "X", (0, -1)), "woe3",
+    ("W", 1, (0, 1)), ("S", 1, "M", (0, 1)), ("W", 1, (0, -1)), ("S", 1, "P", (0, -1)), "qe0", "qe1",
+    ("S", 1, "X", (0, 1)), ("W", 2, (0, 1)), ("S", 2, "M", (0, 1)), ("W", 2, (0, -1)), ("S", 2, "P", (0, -1)),
+    "qe2", "qe3", "maps", ("W", 0, (0, 2)), ("S", 0, "M", (0, 2)), ("W", 0, (0, -2)), ("S", 0, "P", (0, -2)),
+    ("S", 0, "X", (0, 2)), "own", ("S", 0, "X", (0, -2)), ("W", 1, (0, 2)), ("S", 1, "M", (0, 2)),
+    ("W", 1, (0, -2)), ("S", 1, "P", (0, -2)), ("S", 1, "X", (0, 2)), ("W", 2, (0, 2)), ("S", 2, "M", (0, 2)),
+    ("W", 2, (0, -2)), ("S", 2, "P", (0, -2)), ("S", 1, "X", (0, -2)), ("W", 0, (0, 3)), ("S", 0, "M", (0, 3)),
+    ("W", 0, (0, -3)), ("S", 0, "P", (0, -3)), ("W", 0, (1, 2)), ("S", 0, "M", (1, 2)), ("S", 2, "X", (0, 2)),
+    ("W", 1, (0, -3)), ("S", 1, "P", (0, -3)), ("W", 0, (1, -2)), ("S", 0, "P", (1, -2)), ("W", 1, (0, 3)),
+    ("S", 1, "M", (0, 3)), ("S", 2, "X", (0, -2)), ("W", 2, (0, 3)), ("S", 2, "M", (0, 3)), ("W", 2, (0, -3)),
+    ("S", 2, "P", (0, -3)), ("W", 1, (1, 2)), ("S", 1, "M", (1, 2)), ("W", 0, (0, 4, 0)), ("W", 0, (0, 4, 1)),
+    "s00", "s01", ("S", 1, "X", (0, -1)), "s02", ("W", 1, (1, -2)), ("S", 1, "P", (1, -2)), "s03", "sk0", "sx0",
+    ("W", 0, (1, 3)), ("S", 0, "M", (1, 3)), ("W", 1, (0, 4, 0)), ("W", 1, (0, 4, 1)), "g00", ("W", 0, (1, -3)),
+    ("S", 0, "P", (1, -3)), ("W", 2, (1, 2)), ("S", 2, "M", (1, 2)), "g01", ("S", 2, "X", (0, 1)), "g02", "g03",
+    "gx0", ("W", 2, (0, 4, 0)), ("W", 2, (0, 4, 1)), "f00", "f01", ("W", 2, (1, -2)), ("S", 2, "P", (1, -2)),
+    "f02", ("S", 2, "X", (0, -1)), "f03", ("W", 1, (1, 3)), ("S", 1, "M", (1, 3)), ("W", 1, (1, -3)),
+    ("S", 1, "P", (1, -3)), "fk0", "fx0", ("W", 0, (1, 0)), ("W", 0, (1, 1)), ("W", 0, (1, -1)),
+    ("W", 0, (1, 4, 0)), ("W", 0, (1, 4, 1)), "s10", "s11", "s12", "s13", "sk1", "sx1", ("W", 2, (1, 3)),
+    ("S", 2, "M", (1, 3)), ("W", 2, (1, -3)), ("S", 2, "P", (1, -3)), ("W", 1, (1, 0)), ("W", 1, (1, 1)),
+    ("W", 1, (1, -1)), ("W", 1, (1, 4, 0)), ("W", 1, (1, 4, 1)), "g10", "g11", "g12", "g13", "gx1", "sfin",
+    ("W", 2, (1, 0)), ("W", 2, (1, 1)), ("W", 2, (1, -1)), ("W", 2, (1, 4, 0)), ("W", 2, (1, 4, 1)), "f10", "f11",
+    "f12", "f13", "fk1", "fx1", "gfin", "attS", "bwd", "ffin", "attF", "sp11", "sp10", "kvsum", "sp01", "sp00",
+    "rz11", "rx10", "rx01", "rx00", "rz10", "rx11", "rz01", "rz00", "fin1", "rcv1", "fin0", "rcv0",
 ]
 
 
@@ -104,7 +104,8 @@
     loads = {}
     for i, (name, (src, dst)) in enumerate(arrays.items()):
         loads[name] = pltpu.make_async_copy(src, dst, wsem.at[i])
-        loads[name].start()
+        if i < 4:
+            loads[name].start()
 
     barrier = pltpu.get_barrier_semaphore()
     for peer in along + group + [nxt, prv]:
@@ -134,6 +135,10 @@
         copy.start()
         pending.append(copy)
 
+    def drain(keep):
+        while len(pending) > keep:
+            pending.pop(0).wait_send()
+
     def arrived(dst, ssem, rsem, peer):
         pltpu.make_async_remote_copy(
             src_ref=dst, dst_ref=dst, send_sem=ssem, recv_sem=rsem, device_id=peer, device_id_type=MESH
@@ -147,6 +152,8 @@
     put_own(SAVED, normed(saved_ref, 0))
     pl.semaphore_wait(barrier, len(along) + len(group) + 2)
     stage(SAVED)
+    for name in list(arrays)[4:]:
+        loads[name].start()
     loads["grad"].wait()
     put_own(GRAD, grad_ref[...].astype(F32))
     stage(GRAD)
@@ -469,6 +476,7 @@
             out[:, wide(i)] = decode_piece(got, i).astype(BF16)
 
     def finish_forward():
+        drain(40)
         total = reduced(1)
         pack(1, enc_fwd[...] + mapped(total, de), nxt)
         for i in range(16):
@@ -476,6 +484,7 @@
         store(0, out_ref, out_hbm)
 
     def finish_back():
+        drain(40)
         total = reduced(0)
         dots = jnp.sum(total * pull_ref[...], axis=-1, keepdims=True)
         factor = factor_ref[:, :1]
@@ -490,10 +499,12 @@
         store(2, ig_ref, ig_hbm)
 
     def get_grad():
+        drain(4)
         received(0, gs_ref, nxt, s < 7)
         store(3, gs_ref, gs_hbm)
 
     def get_act():
+        drain(4)
         received(1, act_ref, prv, s > 0)
         store(1, act_ref, act_hbm)
 
@@ -541,15 +552,17 @@
                 formed.add(item[1])
                 form_own(item[1])
             hand(*item[1:])
-    for copy in pending:
-        copy.wait_send()
+    drain(0)
     for copy in stores:
         copy.wait()
 
 
 def hand_over(*refs):
-    for i in range(4):
-        refs[4 + i][...] = refs[i][...]
+    copies = [pltpu.make_async_copy(refs[i], refs[4 + i], refs[8].at[i]) for i in range(4)]
+    for copy in copies:
+        copy.start()
+    for copy in copies:
+        copy.wait()
 
 
 def on_device(
@@ -660,7 +673,8 @@
         hand_over,
         out_shape=shapes,
         in_specs=[vmem] * 4,
-        out_specs=[vmem] * 4,
+        out_specs=[hbm] * 4,
+        scratch_shapes=[dma((4,))],
         name="hand_over",
     )(*outs)
     return tuple(o[None] for o in outs)

time: 93.1 us -> 92.2 us (level); the launches traced: 93 us -> 91 us
  Pallas kernels: 92.3 us -> 90.2 us
    pallas_call x1, Pallas kernels: 90.4 us -> 88.2 us  [on_device(): pl.pallas_call(kernel, out_shape=shapes, in_specs=[hbm] * len(operands),...]
where the time goes in v4:
time: 92.2 us; the launch traced here: 91 us
  Pallas kernels  90.2 us (98%)
    pallas_call x1, Pallas kernels, on_device(): pl.pallas_call(kernel, out_shape=shapes, in_specs=[hbm] * len(operands),...  88.2 us
    pallas_call x1, Pallas kernels, on_device(): pl.pallas_call(hand_over, out_shape=shapes, in_specs=[vmem] * 4, out_spec...  1.91 us

profile of v4, /device:TPU:2, one launch (start us, length us, event | category | flops | bytes accessed | tf_op | source)
XLA Modules:
  0.0 91.0 jit_solution(15303284309790169913)
XLA Ops:
  0.6 88.2 %relay_tick.1 = (bf16[8,8192]{1,0:T(8,128)(2,1)}, bf16[8,8192]{1,0:T(8,128)(2,1)}, bf16[8,8192]{1,0:T(8,128)(2,1)}, bf16[8,8192]{1,0:T(8,128)(2,1)}) custom-call(bf16[8,8192]{1,0:T(8,128)(2,1)} %bitcast.23, bf16[8,8192]{1,0:T(8,128)(2,1)} %bitcast.24, bf16[8,8192]{1,0:T(8,128)(2,1)} %bitcast.25, f32[1,8192]{1,0:T(1,128)} %gain_hbm.1, ...), custom_call_target="tpu_custom_call" | custom-call | tf_op jit(solution)/shard_map/relay_tick/pallas_call | solution.py:590
  88.9 1.9 %hand_over.1 = (bf16[8,8192]{1,0:T(8,128)(2,1)}, bf16[8,8192]{1,0:T(8,128)(2,1)}, bf16[8,8192]{1,0:T(8,128)(2,1)}, bf16[8,8192]{1,0:T(8,128)(2,1)}) custom-call(bf16[8,8192]{1,0:T(8,128)(2,1)} %get-tuple-element.12.refs_0_, bf16[8,8192]{1,0:T(8,128)(2,1)} %get-tuple-element.13.refs_1_, bf16[8,8192]{1,0:T(8,128)(2,1)} %get-tuple-element.14.refs_2_, ...), custom_call_target="tpu_custom_call" | custom-call | tf_op jit(solution)/shard_map/hand_over/pallas_call | solution.py:672

commit v5 on v4

--- a/solution.py
+++ b/solution.py
@@ -52,7 +52,8 @@
     ("W", 1, (1, -1)), ("W", 1, (1, 4, 0)), ("W", 1, (1, 4, 1)), "g10", "g11", "g12", "g13", "gx1", "sfin",
     ("W", 2, (1, 0)), ("W", 2, (1, 1)), ("W", 2, (1, -1)), ("W", 2, (1, 4, 0)), ("W", 2, (1, 4, 1)), "f10", "f11",
     "f12", "f13", "fk1", "fx1", "gfin", "attS", "bwd", "ffin", "attF", "sp11", "sp10", "kvsum", "sp01", "sp00",
-    "rz11", "rx10", "rx01", "rx00", "rz10", "rx11", "rz01", "rz00", "fin1", "rcv1", "fin0", "rcv0",
+    "rz11", "rx10", "rx01", "rx00", "rz10", "rx11", "rz01", "rz00",
+    "fin1", "fin0", "outs", "rcv1", "rcv0",
 ]
 
 
@@ -475,13 +476,23 @@
         for i in range(16):
             out[:, wide(i)] = decode_piece(got, i).astype(BF16)
 
+    left = []
+
+    def put_outs():
+        while left:
+            left.pop(0)()
+
     def finish_forward():
         drain(40)
         total = reduced(1)
         pack(1, enc_fwd[...] + mapped(total, de), nxt)
-        for i in range(16):
-            out_ref[:, wide(i)] = (fwd_ref[:, wide(i)].astype(F32) + decode_piece(total, i)).astype(BF16)
-        store(0, out_ref, out_hbm)
+
+        def put_out():
+            for i in range(16):
+                out_ref[:, wide(i)] = (fwd_ref[:, wide(i)].astype(F32) + decode_piece(total, i)).astype(BF16)
+            store(0, out_ref, out_hbm)
+
+        left.append(put_out)
 
     def finish_back():
         drain(40)
@@ -491,12 +502,16 @@
         pull = factor * factor * ((dots[:8] + dots[8:]) * (1.0 / D))
         both = jnp.concatenate([factor, factor], axis=0), jnp.concatenate([pull, pull], axis=0)
         pack(0, enc_grad[...] + both[0] * (mapped(total, dge) - both[1] * enc_saved[...]), prv)
-        for i in range(16):
-            x = saved_ref[:, wide(i)].astype(F32)
-            scaled = decode_piece(total, i) * gain_ref[:, wide(i)]
-            value = grad_ref[:, wide(i)].astype(F32) + factor * (scaled - x * pull)
-            ig_ref[:, wide(i)] = value.astype(BF16)
-        store(2, ig_ref, ig_hbm)
+
+        def put_out():
+            for i in range(16):
+                x = saved_ref[:, wide(i)].astype(F32)
+                scaled = decode_piece(total, i) * gain_ref[:, wide(i)]
+                value = grad_ref[:, wide(i)].astype(F32) + factor * (scaled - x * pull)
+                ig_ref[:, wide(i)] = value.astype(BF16)
+            store(2, ig_ref, ig_hbm)
+
+        left.append(put_out)
 
     def get_grad():
         drain(4)
@@ -522,6 +537,7 @@
         "attF": lambda: attend(1),
         "fin0": finish_back,
         "fin1": finish_forward,
+        "outs": put_outs,
         "rcv0": get_grad,
         "rcv1": get_act,
     }

time: 92.2 us -> 92.2 us (level)
  no operation moved by 1% of the time
where the time goes in v5:
time: 92.2 us; the launch traced here: 91 us
  Pallas kernels  90.2 us (98%)
    pallas_call x1, Pallas kernels, on_device(): pl.pallas_call(kernel, out_shape=shapes, in_specs=[hbm] * len(operands),...  88.2 us
    pallas_call x1, Pallas kernels, on_device(): pl.pallas_call(hand_over, out_shape=shapes, in_specs=[vmem] * 4, out_spec...  1.91 us

profile of v5, /device:TPU:2, one launch (start us, length us, event | category | flops | bytes accessed | tf_op | source)
XLA Modules:
  0.0 91.0 jit_solution(13971994228885269004)
XLA Ops:
  0.6 88.2 %relay_tick.1 = (bf16[8,8192]{1,0:T(8,128)(2,1)}, bf16[8,8192]{1,0:T(8,128)(2,1)}, bf16[8,8192]{1,0:T(8,128)(2,1)}, bf16[8,8192]{1,0:T(8,128)(2,1)}) custom-call(bf16[8,8192]{1,0:T(8,128)(2,1)} %bitcast.23, bf16[8,8192]{1,0:T(8,128)(2,1)} %bitcast.24, bf16[8,8192]{1,0:T(8,128)(2,1)} %bitcast.25, f32[1,8192]{1,0:T(1,128)} %gain_hbm.1, ...), custom_call_target="tpu_custom_call" | custom-call | tf_op jit(solution)/shard_map/relay_tick/pallas_call | solution.py:606
  88.9 1.9 %hand_over.1 = (bf16[8,8192]{1,0:T(8,128)(2,1)}, bf16[8,8192]{1,0:T(8,128)(2,1)}, bf16[8,8192]{1,0:T(8,128)(2,1)}, bf16[8,8192]{1,0:T(8,128)(2,1)}) custom-call(bf16[8,8192]{1,0:T(8,128)(2,1)} %get-tuple-element.12.refs_0_, bf16[8,8192]{1,0:T(8,128)(2,1)} %get-tuple-element.13.refs_1_, bf16[8,8192]{1,0:T(8,128)(2,1)} %get-tuple-element.14.refs_2_, ...), custom_call_target="tpu_custom_call" | custom-call | tf_op jit(solution)/shard_map/hand_over/pallas_call | solution.py:688
